TPU v7x, 256 devices: a whole 4x4x8 slice. The times are simulated.
256 devices in a mesh: cuts: 16 (over x, y_hi, core), fsdp: 16 (over z, y_lo).
Axes of the slice: x: 4, y: 4 (y_hi: 2, y_lo: 2; y = y_hi * 2 + y_lo), z: 8, core: 2. Of those that a mesh axis runs over, the one named last changes fastest.
Arguments:
- layer_input: bfloat16 [131072, 8192], P(('cuts', 'fsdp')), may hold values from -6 to 6
- value_cotangent: bfloat16 [131072, 512], P(('cuts', 'fsdp')), may hold values from -0.015625 to 0.015625
- master_weight: float32 [8192, 512], P('fsdp'), may hold values from -0.0068359375 to 0.0068359375
- first_moment: float32 [8192, 512], P('fsdp'), may hold values from -0.3125 to 0.3125
- second_moment: float32 [8192, 512], P('fsdp'), may hold values from 0.05 to 1
- next_input: bfloat16 [32768, 8192], P(('cuts', 'fsdp')), may hold values from -6 to 6
Outputs:
- new_master: float32 [8192, 512], P('fsdp')
- new_first: float32 [8192, 512], P('fsdp')
- new_second: float32 [8192, 512], P('fsdp')
- next_values: bfloat16 [32768, 512], P(('cuts', 'fsdp'))
All inputs are finite; a program needn't handle non-finite values.
Results may differ from a plain program's by a relative error of at most 0.005.
Values may be sent and summed in bfloat16 or wider, within the bound.
A program may use at most 128 MiB of HBM per device.

v0:
```python
import jax
import jax.numpy as jnp
from jax import lax
from jax.sharding import PartitionSpec as P

STEP = 200


beta_first = 0.9
beta_second = 0.95
learn_rate = 0.001
epsilon = 1e-08


def contract_tokens(source, cotangent):
    return lax.dot_general(
        source, cotangent, (((0,), (0,)), ((), ())), preferred_element_type=jnp.float32
    )


def local(layer_input, value_cotangent, master_weight, first_moment, second_moment, next_input):
    slice_grad = lax.psum_scatter(
        contract_tokens(layer_input, value_cotangent), "fsdp", scatter_dimension=0, tiled=True
    )
    gradient = lax.psum(slice_grad, "cuts")
    new_first = beta_first * first_moment + (1.0 - beta_first) * gradient
    new_second = beta_second * second_moment + (1.0 - beta_second) * gradient * gradient
    first_hat = new_first / (1.0 - beta_first**STEP)
    second_hat = new_second / (1.0 - beta_second**STEP)
    new_master = master_weight - learn_rate * first_hat / (jnp.sqrt(second_hat) + epsilon)
    weight = new_master.astype(jnp.bfloat16)
    values = jnp.dot(
        next_input,
        lax.all_gather(weight, "fsdp", axis=0, tiled=True),
        preferred_element_type=jnp.float32,
    )
    return (new_master, new_first, new_second, values.astype(jnp.bfloat16))


def solution(mesh):
    in_specs = (
        P(("cuts", "fsdp"), None),
        P(("cuts", "fsdp"), None),
        P("fsdp", None),
        P("fsdp", None),
        P("fsdp", None),
        P(("cuts", "fsdp"), None),
    )
    out_specs = (P("fsdp", None), P("fsdp", None), P("fsdp", None), P(("cuts", "fsdp"), None))
    return jax.shard_map(local, mesh=mesh, in_specs=in_specs, out_specs=out_specs, check_vma=False)
```

profile of v0, /device:TPU:1, one launch (start us, length us, event | category | flops | bytes accessed | tf_op | source)
XLA Modules:
  0.0 726.5 jit_solution(13902887335989889412)
XLA Ops:
  7.2 0.0 copy-start
  7.2 0.0 reduce-scatter.2.cloned.1.call-start
  7.2 13.9 %fusion.4 = f32[8192,512]{1,0:T(8,128)} fusion(bf16[512,8192]{1,0:T(8,128)(2,1)} %param.6, bf16[512,512]{1,0:T(8,128)(2,1)} %param.7), kind=kOutput, calls=%fused_computation.7 | convolution fusion | flops 4294967296 | bytes 25690112 | tf_op jit(solution)/shard_map/dot_general | solution.py:16
  21.1 0.0 copy-start.1
  21.1 0.0 reduce-scatter.2.cloned.1.call-update
  21.1 0.0 all-reduce.2.cloned.1.call-start
  21.2 355.4 %reduce-scatter.2.cloned.1.call-done = f32[512,512]{1,0:T(8,128)} async-done(((f32[8192,512]{1,0:T(8,128)}), f32[512,512]{1,0:T(8,128)}) %reduce-scatter.2.cloned.1.call-update) | async-done | bytes 1048592 | tf_op jit(solution)/shard_map/reduce_scatter | solution.py:22
  376.6 0.0 all-reduce.2.cloned.1.call-update
  376.6 0.0 all-gather.2.cloned.1.call-start
  376.7 148.8 %all-reduce.2.cloned.1.call-done = f32[512,512]{1,0:T(8,128)} async-done(((f32[512,512]{1,0:T(8,128)}), f32[512,512]{1,0:T(8,128)}) %all-reduce.2.cloned.1.call-update) | async-done | bytes 1048592 | tf_op jit(solution)/shard_map/psum | solution.py:25
  525.4 0.0 copy-done.1
  525.4 4.2 fusion.2
  529.6 0.0 all-gather.2.cloned.1.call-update
  529.7 183.8 %all-gather.2.cloned.1.call-done = bf16[8192,512]{1,0:T(8,128)(2,1)} async-done(((bf16[512,512]{1,0:T(8,128)(2,1)}), bf16[8192,512]{1,0:T(8,128)(2,1)}) %all-gather.2.cloned.1.call-update) | async-done | bytes 8388624 | tf_op jit(solution)/shard_map/all_gather | solution.py:34
  713.5 0.0 copy-done
  713.5 5.8 fusion
  719.2 0.8 copy.10
Async XLA Ops:
  7.2 706.3 %copy-start = (bf16[128,8192]{1,0:T(8,128)(2,1)S(1)}, bf16[128,8192]{1,0:T(8,128)(2,1)}, u32[]{:S(2)}) copy-start(bf16[128,8192]{1,0:T(8,128)(2,1)} %param.11) | copy-start | bytes 6291460
  7.2 369.4 %reduce-scatter.2.cloned.1.call-start = ((), (), s32[]{:S(2)}) async-start(), calls=%async_computation.1 | async-start | bytes 17825792 | tf_op jit(solution)/shard_map/reduce_scatter | solution.py:22
  21.1 504.3 %copy-start.1 = (f32[512,512]{1,0:T(8,128)S(1)}, f32[512,512]{1,0:T(8,128)}, u32[]{:S(2)}) copy-start(f32[512,512]{1,0:T(8,128)} %param.8) | copy-start | bytes 3145732
  21.1 504.3 %all-reduce.2.cloned.1.call-start = ((), (), s32[]{:S(2)}) async-start(), calls=%async_computation.2 | async-start | bytes 2097152 | tf_op jit(solution)/shard_map/psum | solution.py:25
  376.6 336.8 %all-gather.2.cloned.1.call-start = ((), (), s32[]{:S(2)}) async-start(), calls=%async_computation.3 | async-start | bytes 8912896 | tf_op jit(solution)/shard_map/all_gather | solution.py:34
Sparse Core Ops, SparseCore 0:
  21.2 355.3 reduce-scatter.1
  379.2 146.1 all-reduce.1
  529.8 183.6 all-gather.1
where the time goes:
time: 727 us
  waiting for transfers between devices  688 us (95%)
  matrix products  19.6 us (3%)
  between operations  13.8 us (2%)
    reduce_scatter x1, waiting for transfers between devices, local(): lax.psum_scatter(contract_tokens(layer_input, value_cotangent), 'fsdp', s...  355 us
    all_gather x1, waiting for transfers between devices, local(): lax.all_gather(weight, 'fsdp', axis=0, tiled=True)  184 us
    psum x1, waiting for transfers between devices, local(): gradient = lax.psum(slice_grad, 'cuts')  149 us
  transfers between devices with their start and end apart: 3, of which 3 were waited for; matrix products, arithmetic and copies ran while one was open for 0% of the time, Pallas kernels for 0%

commit v1 on v0

v1 whole, which is shorter than its diff:
```python
import functools

import jax
import jax.numpy as jnp
from jax import lax
from jax.experimental import pallas as pl
from jax.experimental.pallas import tpu as pltpu
from jax.sharding import PartitionSpec as P

STEP = 200
beta_first = 0.9
beta_second = 0.95
learn_rate = 0.001
epsilon = 1e-08

MESH = pl.DeviceIdType.MESH
BF16 = jnp.bfloat16
F32 = jnp.float32

NX, NY, NZ = 4, 4, 8
AXES = {"x": NX, "y": NY, "z": NZ}
ORDER = (4, 3, 5, 2, 6, 1, 7, 0)
PLACE = {r: k for k, r in enumerate(ORDER)}
UNITS = [(row, col) for row in range(2) for col in range(4)]
STREAM_UNITS = {"x": UNITS[0:3], "y": UNITS[3:6], "z": UNITS[6:8]}


def position():
    cuts, fsdp = lax.axis_index("cuts"), lax.axis_index("fsdp")
    x, y_hi, core = cuts // 4, lax.rem(cuts // 2, 2), lax.rem(cuts, 2)
    z, y_lo = fsdp // 2, lax.rem(fsdp, 2)
    return x, y_hi * 2 + y_lo, z, core


def device(x, y, z, core):
    return (x * 4 + (y // 2) * 2 + core, z * 2 + lax.rem(y, 2))


def kernel(
    x_hbm, c_hbm, master_hbm, first_hbm, second_hbm, next_hbm,
    o_master, o_first, o_second, o_values,
    XB, CB, NB, PX, PY, PZ,
    RXL, RXS, RYL, RYS, RZL, RZS,
    S2X, S2Y, S2Z, R2X, R2Y, R2Z, S3X, S3Y, S3Z, R3X, R3Y, R3Z,
    WX, WY, WZ, GB, MB, FB, SB, WT, VO, VS, VR, VALS,
    load_sem, send_sem, recv_sem, big_send, big_recv,
):
    x, y, z, core = position()
    here = {"x": x, "y": y, "z": z}

    def towards(axis, delta):
        at = dict(here)
        at[axis] = lax.rem(here[axis] + delta, AXES[axis])
        return device(at["x"], at["y"], at["z"], core)

    mate = device(x, y, z, 1 - core)

    counts = {"load": 0, "remote": 0}
    sends = []

    def local(src, dst):
        copy = pltpu.make_async_copy(src, dst, load_sem.at[counts["load"]])
        counts["load"] += 1
        copy.start()
        return copy

    def push(src, dst, dev):
        slot = counts["remote"]
        counts["remote"] += 1
        copy = pltpu.make_async_remote_copy(
            src_ref=src, dst_ref=dst, send_sem=send_sem.at[slot], recv_sem=recv_sem.at[slot],
            device_id=dev, device_id_type=MESH,
        )
        copy.start()
        sends.append(copy)
        return copy

    def block_of(t):
        k = t // 2
        odd = lax.rem(k, 2)
        r = 4 + (1 - odd) * (k // 2) - odd * ((k + 1) // 2)
        return lax.rem(z + r, NZ) * 2 + lax.rem(t, 2)

    def columns(t, side):
        return pl.ds(pl.multiple_of(block_of(t) * 512 + side * 256, 256), 256)

    def x_load(t):
        return pltpu.make_async_copy(
            x_hbm.at[:, columns(t, core)], XB.at[t, pl.ds(0, 512)], big_send.at[32 + t])

    def x_push(t):
        return pltpu.make_async_remote_copy(
            src_ref=x_hbm.at[:, columns(t, 1 - core)], dst_ref=XB.at[t, pl.ds(512, 512)],
            send_sem=big_send.at[t], recv_sem=big_recv.at[t], device_id=mate, device_id_type=MESH)

    def n_load(t):
        return pltpu.make_async_copy(
            next_hbm.at[:, columns(t, core)], NB.at[t, pl.ds(0, 128)], big_send.at[48 + t])

    def n_push(t):
        return pltpu.make_async_remote_copy(
            src_ref=next_hbm.at[:, columns(t, 1 - core)], dst_ref=NB.at[t, pl.ds(128, 128)],
            send_sem=big_send.at[16 + t], recv_sem=big_recv.at[16 + t], device_id=mate, device_id_type=MESH)

    def each(n, act):
        def body(t, carry):
            act(t)
            return carry
        lax.fori_loop(0, n, body, 0)

    c_own = local(c_hbm, CB.at[pl.ds(0, 512)])
    each(16, lambda t: x_load(t).start())

    barrier = pltpu.get_barrier_semaphore()
    partners = [mate] + [towards(a, d) for a in "xyz" for d in range(1, AXES[a])]
    for dev in partners:
        pl.semaphore_signal(barrier, inc=1, device_id=dev, device_id_type=MESH)
    pl.semaphore_wait(barrier, len(partners))

    c_mate = push(c_hbm, CB.at[pl.ds(512, 512)], mate)
    each(16, lambda t: x_push(t).start())
    m_own = local(master_hbm, MB)
    f_own = local(first_hbm, FB)
    s_own = local(second_hbm, SB)
    each(16, lambda t: n_load(t).start())
    each(16, lambda t: n_push(t).start())

    def blocks():
        def make(y_lo):
            out = []
            for g in range(8):
                xa, y_hi = g // 2, g % 2
                xr = lax.rem(xa + NX - x, NX)
                yr = lax.rem(y_hi * 2 + y_lo + NY - y, NY)
                out.append((g, xr, yr))
            return out
        return make

    groups = blocks()

    def tile(t, carry):
        x_load(t).wait()
        x_push(t).wait_recv()
        g_tile = lax.dot_general(
            XB[t], CB[...], (((0,), (0,)), ((), ())), preferred_element_type=F32).astype(BF16)
        k, y_lo = t // 2, lax.rem(t, 2)
        h, kk = k // 4, lax.rem(k, 4)
        for g, xr, yr in groups(y_lo):
            for i, (row, col) in enumerate(STREAM_UNITS["x"]):
                PX[xr, h, yr, kk, i] = g_tile[g * 32 + row * 16:g * 32 + row * 16 + 16, col * 128:col * 128 + 128]
            for i, (row, col) in enumerate(STREAM_UNITS["y"]):
                PY[yr, h, xr, kk, i] = g_tile[g * 32 + row * 16:g * 32 + row * 16 + 16, col * 128:col * 128 + 128]
            for i, (row, col) in enumerate(STREAM_UNITS["z"]):
                PZ[k, xr, yr, i] = g_tile[g * 32 + row * 16:g * 32 + row * 16 + 16, col * 128:col * 128 + 128]
        return carry

    def gemm(first, last):
        lax.fori_loop(first * 2, last * 2, tile, 0)

    def add_rows(dst, terms, n):
        def body(i, carry):
            total = terms[0][i].astype(F32)
            for term in terms[1:]:
                total = total + term[i].astype(F32)
            dst[i] = total.astype(dst.dtype)
            return carry
        lax.fori_loop(0, n, body, 0)

    class Ring:
        def __init__(self, axis, chunk, long_buf, short_buf, rows):
            self.axis, self.chunk, self.long_buf, self.short_buf, self.rows = axis, chunk, long_buf, short_buf, rows
            self.n = AXES[axis]
            self.long, self.short = {}, {}

        def _send(self, way, dist, half, buf, step):
            n = self.n
            r = dist if way == 0 else n - dist
            dev = towards(self.axis, 1 if way == 0 else n - 1)
            return push(self.chunk(r, half), buf.at[way, step], dev)

        def send_long(self, way, step):
            dist = self.n // 2 - step
            if step > 0:
                self.long[way, step - 1].wait_recv()
                r = dist if way == 0 else self.n - dist
                c = self.chunk(r, way)
                add_rows(c, [c, self.long_buf.at[way, step - 1]], self.rows)
            self.long[way, step] = self._send(way, dist, way, self.long_buf, step)

        def send_short(self, way, step):
            dist = self.n // 2 - 1 - step
            if step > 0:
                self.short[way, step - 1].wait_recv()
                r = dist if way == 0 else self.n - dist
                c = self.chunk(r, 1 - way)
                add_rows(c, [c, self.short_buf.at[way, step - 1]], self.rows)
            self.short[way, step] = self._send(way, dist, 1 - way, self.short_buf, step)

        def finish(self):
            n = self.n
            out = []
            for way in range(2):
                self.long[way, n // 2 - 1].wait_recv()
                self.short[way, n // 2 - 2].wait_recv()
            for half in range(2):
                out.append([
                    self.chunk(0, half),
                    self.long_buf.at[half, n // 2 - 1],
                    self.short_buf.at[1 - half, n // 2 - 2],
                ])
            return out

    ring_x = Ring("x", lambda r, h: PX.at[r, h], RXL, RXS, 4)
    ring_y = Ring("y", lambda r, h: PY.at[r, h], RYL, RYS, 4)
    ring_z = Ring("z", lambda r, h: PZ.at[PLACE[r], pl.ds(2 * h, 2)], RZL, RZS, 2)

    c_own.wait()
    c_mate.wait_recv()
    gemm(0, 1)
    ring_z.send_long(0, 0)
    ring_z.send_long(1, 0)
    gemm(1, 3)
    ring_z.send_short(0, 0)
    ring_z.send_short(1, 0)
    gemm(3, 4)
    ring_x.send_long(0, 0)
    ring_y.send_long(0, 0)
    ring_x.send_short(1, 0)
    ring_y.send_short(1, 0)
    ring_z.send_long(0, 1)
    ring_z.send_long(1, 1)
    gemm(4, 8)
    ring_x.send_long(1, 0)
    ring_y.send_long(1, 0)
    ring_x.send_short(0, 0)
    ring_y.send_short(0, 0)
    for way in range(2):
        ring_z.send_short(way, 1)
    for way in range(2):
        ring_z.send_long(way, 2)
    for way in range(2):
        ring_x.send_long(way, 1)
        ring_y.send_long(way, 1)
    for way in range(2):
        ring_z.send_short(way, 2)
    for way in range(2):
        ring_z.send_long(way, 3)

    def spread(axis, src, dst):
        n = AXES[axis]
        far_first = sorted(range(1, n), key=lambda r: -min(r, n - r))
        return [push(src(r), dst(r), towards(axis, r)) for r in far_first]

    def settle(copies):
        for copy in copies:
            copy.wait_recv()

    def ring_total_xy(ring, S):
        for half, terms in enumerate(ring.finish()):
            def body(i, carry, half=half, terms=terms):
                total = terms[0][i].astype(F32) + terms[1][i].astype(F32) + terms[2][i].astype(F32)
                S[i, pl.ds(4 * half, 4)] = total.astype(BF16)
                return carry
            lax.fori_loop(0, 4, body, 0)

    for half, terms in enumerate(ring_z.finish()):
        def body(i, carry, half=half, terms=terms):
            total = terms[0][i].astype(F32) + terms[1][i].astype(F32) + terms[2][i].astype(F32)
            S2Z[2 * half + i] = total.astype(BF16)
            return carry
        lax.fori_loop(0, 2, body, 0)
    z2 = spread("x", lambda r: S2Z.at[r], lambda r: R2Z.at[r - 1])
    ring_total_xy(ring_x, S2X)
    x2 = spread("y", lambda r: S2X.at[r], lambda r: R2X.at[r - 1])
    ring_total_xy(ring_y, S2Y)
    y2 = spread("x", lambda r: S2Y.at[r], lambda r: R2Y.at[r - 1])

    settle(z2)
    add_rows(S3Z, [S2Z.at[0], R2Z.at[0], R2Z.at[1], R2Z.at[2]], 4)
    z3 = spread("y", lambda r: S3Z.at[r], lambda r: R3Z.at[r - 1])
    settle(x2)
    add_rows(S3X, [S2X.at[0], R2X.at[0], R2X.at[1], R2X.at[2]], 8)
    x3 = spread("z", lambda r: S3X.at[PLACE[r]], lambda r: R3X.at[r - 1])
    settle(y2)
    add_rows(S3Y, [S2Y.at[0], R2Y.at[0], R2Y.at[1], R2Y.at[2]], 8)
    y3 = spread("z", lambda r: S3Y.at[PLACE[r]], lambda r: R3Y.at[r - 1])

    m_own.wait()
    f_own.wait()
    s_own.wait()

    def adam(gradient, master, first, second):
        new_first = beta_first * first + (1.0 - beta_first) * gradient
        new_second = beta_second * second + (1.0 - beta_second) * gradient * gradient
        first_hat = new_first / (1.0 - beta_first**STEP)
        second_hat = new_second / (1.0 - beta_second**STEP)
        new_master = master - learn_rate * first_hat / (jnp.sqrt(second_hat) + epsilon)
        return new_master, new_first, new_second

    y_hi = y // 2
    own_row = core * 256 + x * 64 + y_hi * 32

    def own_update(stream, own, received, n, put):
        for i, (row, col) in enumerate(STREAM_UNITS[stream]):
            gradient = own[i].astype(F32)
            for s in range(n):
                gradient = gradient + received[s, i].astype(F32)
            gradient = gradient.astype(BF16)
            GB[0, 0, 0, row * 16:row * 16 + 16, col * 128:col * 128 + 128] = gradient
            rows = pl.ds(pl.multiple_of(own_row + row * 16, 16), 16)
            cols = slice(col * 128, col * 128 + 128)
            new_master, _, _ = adam(gradient.astype(F32), MB[rows, cols], FB[rows, cols], SB[rows, cols])
            put(i, new_master.astype(BF16))

    def put_x(i, w):
        WX[0, 0, 7, i] = w

    def put_y(i, w):
        WY[0, 0, 7, i] = w

    def put_z(i, w):
        WZ[7, 0, 0, i] = w

    settle(z3)
    own_update("z", S3Z.at[0], R3Z, 3, put_z)
    wz1 = spread("y", lambda r: WZ.at[7, 0, 0], lambda r: WZ.at[7, 0, NY - r])
    settle(x3)
    own_update("x", S3X.at[7], R3X, 7, put_x)
    wx1 = spread("z", lambda r: WX.at[0, 0, 7], lambda r: WX.at[0, 0, PLACE[NZ - r]])
    settle(y3)
    own_update("y", S3Y.at[7], R3Y, 7, put_y)
    wy1 = spread("z", lambda r: WY.at[0, 0, 7], lambda r: WY.at[0, 0, PLACE[NZ - r]])
    g1 = spread("x", lambda r: GB.at[0, 0, 0], lambda r: GB.at[0, 0, NX - r])

    settle(wz1)
    wz2 = spread("x", lambda r: WZ.at[7, 0], lambda r: WZ.at[7, NX - r])
    settle(wx1)
    wx2 = spread("y", lambda r: WX.at[0, 0], lambda r: WX.at[0, NY - r])
    settle(wy1)
    wy2 = spread("x", lambda r: WY.at[0, 0], lambda r: WY.at[0, NX - r])

    class Gather:
        def __init__(self, axis, chunk):
            self.axis, self.chunk, self.n = axis, chunk, AXES[axis]
            self.long, self.short = {}, {}

        def _send(self, way, step, half):
            n = self.n
            r = (n - step) % n if way == 0 else step
            land = (n - step - 1) % n if way == 0 else (step + 1) % n
            return push(self.chunk(r, half), self.chunk(land, half), towards(self.axis, 1 if way == 0 else n - 1))

        def send_long(self, way, step):
            if step > 0:
                self.long[way, step - 1].wait_recv()
            self.long[way, step] = self._send(way, step, way)

        def send_short(self, way, step):
            if step > 0:
                self.short[way, step - 1].wait_recv()
            self.short[way, step] = self._send(way, step, 1 - way)

        def finish(self):
            for way in range(2):
                self.long[way, self.n // 2 - 1].wait_recv()
                self.short[way, self.n // 2 - 2].wait_recv()

    gather_x = Gather("x", lambda r, h: WX.at[r, pl.ds(2 * h, 2)])
    gather_y = Gather("y", lambda r, h: WY.at[r, pl.ds(2 * h, 2)])
    gather_z = Gather("z", lambda r, h: WZ.at[PLACE[r], pl.ds(2 * h, 2)])

    settle(wz2)
    for way in range(2):
        gather_z.send_long(way, 0)
        gather_z.send_short(way, 0)
    settle(wx2)
    for way in range(2):
        gather_x.send_long(way, 0)
    for way in range(2):
        gather_x.send_short(way, 0)
    settle(wy2)
    for way in range(2):
        gather_y.send_long(way, 0)
    for way in range(2):
        gather_y.send_short(way, 0)

    settle(g1)
    g2 = push(GB.at[0, 0], GB.at[0, 1], towards("y", 2))

    for way in range(2):
        gather_z.send_long(way, 1)
        gather_z.send_short(way, 1)
    for way in range(2):
        gather_x.send_long(way, 1)
        gather_y.send_long(way, 1)
    for way in range(2):
        gather_z.send_long(way, 2)
        gather_z.send_short(way, 2)
    g2.wait_recv()
    g3 = push(GB.at[0], GB.at[1], mate)
    for way in range(2):
        gather_z.send_long(way, 3)

    def moments(cr):
        def body(i, carry):
            yr, xr = i // 4, lax.rem(i, 4)
            side = core if cr == 0 else 1 - core
            row = side * 256 + lax.rem(x + xr, NX) * 64 + lax.rem(y_hi + yr, 2) * 32
            rows = pl.ds(pl.multiple_of(row, 32), 32)
            new_master, new_first, new_second = adam(
                GB[cr, yr, xr].astype(F32), MB[rows, :], FB[rows, :], SB[rows, :])
            MB[rows, :] = new_master
            FB[rows, :] = new_first
            SB[rows, :] = new_second
            return carry
        lax.fori_loop(0, 8, body, 0)

    moments(0)
    g3.wait_recv()
    moments(1)
    outs = [local(MB, o_master), local(FB, o_first), local(SB, o_second)]

    each(16, lambda t: n_load(t).wait())
    each(16, lambda t: n_push(t).wait_recv())
    gather_z.finish()
    gather_x.finish()
    gather_y.finish()

    VO[...] = jnp.zeros_like(VO)

    def value_tile(t, carry):
        k, y_lo = t // 2, lax.rem(t, 2)
        for g, xr, yr in groups(y_lo):
            def at(row, col):
                return (pl.ds(g * 32 + row * 16, 16), pl.ds(col * 128, 128))
            for i, (row, col) in enumerate(STREAM_UNITS["x"]):
                WT[at(row, col)] = WX[xr, yr, k, i]
            for i, (row, col) in enumerate(STREAM_UNITS["y"]):
                WT[at(row, col)] = WY[yr, xr, k, i]
            for i, (row, col) in enumerate(STREAM_UNITS["z"]):
                WT[at(row, col)] = WZ[k, xr, yr, i]
        VO[...] += jnp.dot(NB[t], WT[...], preferred_element_type=F32)
        return carry

    lax.fori_loop(0, 16, value_tile, 0)
    VS[...] = VO[pl.ds(128, 128), :]
    v_mate = push(VS, VR, mate)
    v_mate.wait_recv()
    VALS[...] = (VO[pl.ds(0, 128), :] + VR[...]).astype(BF16)
    outs.append(local(VALS, o_values))

    for copy in outs:
        copy.wait()
    for copy in sends:
        copy.wait_send()
    each(16, lambda t: x_push(t).wait_send())
    each(16, lambda t: n_push(t).wait_send())


def local_step(layer_input, value_cotangent, master_weight, first_moment, second_moment, next_input):
    unit = (16, 128)
    vm = lambda shape, dtype=BF16: pltpu.VMEM(shape, dtype)
    half_xy = (4, 4, 3) + unit
    half_z = (2, 4, 2) + unit
    scratch = [
        vm((16, 1024, 256)), vm((1024, 512)), vm((16, 256, 256)),
        vm((4, 2, 4, 4, 3) + unit), vm((4, 2, 4, 4, 3) + unit), vm((8, 4, 4, 2) + unit),
        vm((2, 2) + half_xy), vm((2, 1) + half_xy),
        vm((2, 2) + half_xy), vm((2, 1) + half_xy),
        vm((2, 4) + half_z), vm((2, 3) + half_z),
        vm((4, 8, 3) + unit), vm((4, 8, 3) + unit), vm((4, 4, 2) + unit),
        vm((3, 8, 3) + unit), vm((3, 8, 3) + unit), vm((3, 4, 2) + unit),
        vm((8, 3) + unit), vm((8, 3) + unit), vm((4, 2) + unit),
        vm((7, 3) + unit), vm((7, 3) + unit), vm((3, 2) + unit),
        vm((4, 4, 8, 3) + unit), vm((4, 4, 8, 3) + unit), vm((8, 4, 4, 2) + unit),
        vm((2, 2, 4, 32, 512)),
        vm((512, 512), F32), vm((512, 512), F32), vm((512, 512), F32),
        vm((256, 512)), vm((256, 512), F32), vm((128, 512), F32), vm((128, 512), F32), vm((128, 512)),
        pltpu.SemaphoreType.DMA((8,)), pltpu.SemaphoreType.DMA((128,)), pltpu.SemaphoreType.DMA((128,)),
        pltpu.SemaphoreType.DMA((64,)), pltpu.SemaphoreType.DMA((32,)),
    ]
    any_spec = pl.BlockSpec(memory_space=pl.ANY)
    return tuple(pl.pallas_call(
        kernel,
        out_shape=(
            jax.ShapeDtypeStruct((512, 512), F32),
            jax.ShapeDtypeStruct((512, 512), F32),
            jax.ShapeDtypeStruct((512, 512), F32),
            jax.ShapeDtypeStruct((128, 512), BF16),
        ),
        in_specs=[any_spec] * 6,
        out_specs=(any_spec,) * 4,
        scratch_shapes=scratch,
        compiler_params=pltpu.CompilerParams(
            collective_id=0, has_side_effects=True, vmem_limit_bytes=60 * 2**20),
        cost_estimate=pl.CostEstimate(flops=5_400_000_000, bytes_accessed=18_000_000, transcendentals=0),
        name="value_projection_step",
    )(layer_input, value_cotangent, master_weight, first_moment, second_moment, next_input))


def solution(mesh):
    in_specs = (
        P(("cuts", "fsdp"), None),
        P(("cuts", "fsdp"), None),
        P("fsdp", None),
        P("fsdp", None),
        P("fsdp", None),
        P(("cuts", "fsdp"), None),
    )
    out_specs = (P("fsdp", None), P("fsdp", None), P("fsdp", None), P(("cuts", "fsdp"), None))
    return jax.shard_map(local_step, mesh=mesh, in_specs=in_specs, out_specs=out_specs, check_vma=False)
```

time: 727 us -> 92.4 us (0.13)
  waiting for transfers between devices: 688 us -> 0 us
  Pallas kernels: 0 us -> 83.2 us
  matrix products: 19.6 us -> 0 us
  between operations: 13.8 us -> 0.64 us
  local copies, waits for them, and re-layouts: 0.78 us -> 8.35 us
    reduce_scatter x1 -> x0, waiting for transfers between devices: 355 us -> none  [local(): lax.psum_scatter(contract_tokens(layer_input, value_cotangent), 'fsdp', s...]
    all_gather x1 -> x0, waiting for transfers between devices: 184 us -> none  [local(): lax.all_gather(weight, 'fsdp', axis=0, tiled=True)]
    psum x1 -> x0, waiting for transfers between devices: 149 us -> none  [local(): gradient = lax.psum(slice_grad, 'cuts')]
    pallas_call x0 -> x1, Pallas kernels: none -> 83.2 us  [local_step(): pl.pallas_call(kernel, out_shape=(jax.ShapeDtypeStruct((512, 512), F32),...]
    dot_general x2 -> x0, matrix products: 19.6 us -> none  [the longest x1 13.9 us: contract_tokens(): lax.dot_general(source, cotangent, (((0,), (0,)), ((), ())), preferred_el...]
    unnamed x5 -> x4, local copies, waits for them, and re-layouts: 0.78 us -> 8.35 us
  transfers between devices with their start and end apart: 3 -> 0, of which waited for: 3 -> 0; matrix products, arithmetic and copies ran while one was open for 0% -> 0% of each run, Pallas kernels for 0% -> 0%
where the time goes in v1:
time: 92.4 us; the launch traced here: 92.2 us
  Pallas kernels  83.2 us (90%)
  local copies, waits for them, and re-layouts  8.35 us (9%)
    pallas_call x1, Pallas kernels, local_step(): pl.pallas_call(kernel, out_shape=(jax.ShapeDtypeStruct((512, 512), F32),...  83.2 us
    unnamed x4, local copies, waits for them, and re-layouts  8.35 us

profile of v1, /device:TPU:1, one launch (start us, length us, event | category | flops | bytes accessed | tf_op | source)
XLA Modules:
  0.0 92.2 jit_solution(7989066321984536042)
XLA Ops:
  0.6 83.2 %value_projection_step.1 = (f32[512,512]{1,0:T(8,128)}, f32[512,512]{1,0:T(8,128)}, f32[512,512]{1,0:T(8,128)}, bf16[128,512]{1,0:T(8,128)(2,1)}) custom-call(bf16[512,8192]{1,0:T(8,128)(2,1)} %x_hbm.1, bf16[512,512]{1,0:T(8,128)(2,1)} %c_hbm.1, f32[512,512]{1,0:T(8,128)} %master_hbm.1, f32[512,512]{1,0:T(8,128)} %first_hbm.1, f32[512,512]{1,0:T(8,128)} %second_hbm.1, ...), custom_call_target="tpu_custom_call" | custom-call | flops 5400000000 | bytes 18000000 | tf_op jit(solution)/shard_map/value_projection_step/pallas_call | solution.py:483
  83.8 2.3 %copy.14 = f32[512,512]{1,0:T(8,128)} copy(f32[512,512]{1,0:T(8,128)} %get-tuple-element.8) | data formatting | bytes 2097152
  86.1 2.3 %copy.15 = f32[512,512]{1,0:T(8,128)} copy(f32[512,512]{1,0:T(8,128)} %get-tuple-element.9) | data formatting | bytes 2097152
  88.3 2.3 %copy.16 = f32[512,512]{1,0:T(8,128)} copy(f32[512,512]{1,0:T(8,128)} %get-tuple-element.10) | data formatting | bytes 2097152
  90.6 1.6 %copy.17 = bf16[128,512]{1,0:T(8,128)(2,1)} copy(bf16[128,512]{1,0:T(8,128)(2,1)} %get-tuple-element.11) | data formatting | bytes 262144

commit v2 on v0

v2 whole, which is shorter than its diff:
```python
import functools

import jax
import jax.numpy as jnp
from jax import lax
from jax.experimental import pallas as pl
from jax.experimental.pallas import tpu as pltpu
from jax.sharding import PartitionSpec as P

STEP = 200
beta_first = 0.9
beta_second = 0.95
learn_rate = 0.001
epsilon = 1e-08

MESH = pl.DeviceIdType.MESH
BF16 = jnp.bfloat16
F32 = jnp.float32

NX, NY, NZ = 4, 4, 8
AXES = {"x": NX, "y": NY, "z": NZ}
ORDER = (4, 3, 5, 2, 6, 1, 7, 0)
PLACE = {r: k for k, r in enumerate(ORDER)}
SLOTS = 232
UNITS = [(row, col) for row in range(2) for col in range(4)]
Q = 4
K = NZ // Q
STREAM_UNITS = {"x": UNITS[0:3], "y": UNITS[3:6], "z": UNITS[6:8]}


def position():
    cuts, fsdp = lax.axis_index("cuts"), lax.axis_index("fsdp")
    x, y_hi, core = cuts // 4, lax.rem(cuts // 2, 2), lax.rem(cuts, 2)
    z, y_lo = fsdp // 2, lax.rem(fsdp, 2)
    return x, y_hi * 2 + y_lo, z, core


def device(x, y, z, core):
    return (x * 4 + (y // 2) * 2 + core, z * 2 + lax.rem(y, 2))


def kernel(
    x_hbm, c_hbm, master_hbm, first_hbm, second_hbm, next_hbm,
    o_master, o_first, o_second, o_values,
    XB, CB, NB, PX, PY, PZ,
    RXL, RXS, RYL, RYS, RZL, RZS,
    S2X, S2Y, S2Z, R2X, R2Y, R2Z, S3X, S3Y, S3Z, R3X, R3Y, R3Z,
    WX, WY, WZ, GB, MB, FB, SB, WT, VO, VS, VR,
    load_sem, send_sem, recv_sem, big_send, big_recv,
):
    x, y, z, core = position()
    here = {"x": x, "y": y, "z": z}

    def towards(axis, delta):
        at = dict(here)
        at[axis] = lax.rem(here[axis] + delta, AXES[axis])
        return device(at["x"], at["y"], at["z"], core)

    mate = device(x, y, z, 1 - core)
    ahead = {(a, d): towards(a, d) for a in "xyz" for d in range(1, AXES[a])}

    barrier = pltpu.get_barrier_semaphore()
    partners = [mate] + [ahead[key] for key in sorted(ahead, key=lambda p: -min(p[1], AXES[p[0]] - p[1]))]
    for dev in partners:
        pl.semaphore_signal(barrier, inc=1, device_id=dev, device_id_type=MESH)

    counts = {"load": 0, "remote": 0}
    sends = []

    def local(src, dst):
        copy = pltpu.make_async_copy(src, dst, load_sem.at[counts["load"]])
        counts["load"] += 1
        copy.start()
        return copy

    class Push:
        def __init__(self, src, dst, dev):
            slot = counts["remote"]
            counts["remote"] += 1
            self.copy = pltpu.make_async_remote_copy(
                src_ref=src, dst_ref=dst, send_sem=send_sem.at[slot], recv_sem=recv_sem.at[slot],
                device_id=dev, device_id_type=MESH,
            )
            self.copy.start()
            self.landed = False
            sends.append(self)

        def arrive(self):
            if not self.landed:
                self.landed = True
                self.copy.wait_recv()

    push = Push

    def block_of(t):
        k = t // 2
        odd = lax.rem(k, 2)
        r = 4 + (1 - odd) * (k // 2) - odd * ((k + 1) // 2)
        return lax.rem(z + r, NZ) * 2 + lax.rem(t, 2)

    def columns(t, side):
        return pl.ds(pl.multiple_of(block_of(t) * 512 + side * 256, 256), 256)

    def x_load(t):
        return pltpu.make_async_copy(
            x_hbm.at[:, columns(t, core)], XB.at[t, pl.ds(0, 512)], big_send.at[32 + t])

    def x_push(t):
        return pltpu.make_async_remote_copy(
            src_ref=x_hbm.at[:, columns(t, 1 - core)], dst_ref=XB.at[t, pl.ds(512, 512)],
            send_sem=big_send.at[t], recv_sem=big_recv.at[t], device_id=mate, device_id_type=MESH)

    def n_place(t, rows):
        return NB.at[t // 4, pl.ds(rows, 128), pl.ds(pl.multiple_of(lax.rem(t, 4) * 256, 256), 256)]

    def n_load(t):
        return pltpu.make_async_copy(next_hbm.at[:, columns(t, core)], n_place(t, 0), big_send.at[48 + t])

    def n_push(t):
        return pltpu.make_async_remote_copy(
            src_ref=next_hbm.at[:, columns(t, 1 - core)], dst_ref=n_place(t, 128),
            send_sem=big_send.at[16 + t], recv_sem=big_recv.at[16 + t], device_id=mate, device_id_type=MESH)

    def each(n, act):
        def body(t, carry):
            act(t)
            return carry
        lax.fori_loop(0, n, body, 0)

    c_own = local(c_hbm, CB.at[pl.ds(0, 512)])
    each(16, lambda t: x_load(t).start())
    pl.semaphore_wait(barrier, len(partners))

    c_mate = push(c_hbm, CB.at[pl.ds(512, 512)], mate)
    each(16, lambda t: x_push(t).start())
    m_own = local(master_hbm, MB)
    f_own = local(first_hbm, FB)
    s_own = local(second_hbm, SB)
    each(16, lambda t: n_load(t).start())
    each(16, lambda t: n_push(t).start())

    def groups(y_lo):
        out = []
        for g in range(8):
            xr = lax.rem(g // 2 + NX - x, NX)
            yr = lax.rem((g % 2) * 2 + y_lo + NY - y, NY)
            out.append((g, xr, yr))
        return out

    def tile(t, carry):
        x_load(t).wait()
        x_push(t).wait_recv()
        g_tile = lax.dot_general(
            XB[t], CB[...], (((0,), (0,)), ((), ())), preferred_element_type=F32).astype(BF16)
        k, y_lo = t // 2, lax.rem(t, 2)
        q, kk = k // K, lax.rem(k, K)

        def piece(g, unit):
            row, col = unit
            return g_tile[g * 32 + row * 16:g * 32 + row * 16 + 16, col * 128:col * 128 + 128]

        for g, xr, yr in groups(y_lo):
            for i, unit in enumerate(STREAM_UNITS["x"]):
                PX[xr, q, yr, kk, i] = piece(g, unit)
            for i, unit in enumerate(STREAM_UNITS["y"]):
                PY[yr, q, xr, kk, i] = piece(g, unit)
            for i, unit in enumerate(STREAM_UNITS["z"]):
                PZ[k, xr, yr, i] = piece(g, unit)
        return carry

    def gemm(first, last):
        lax.fori_loop(first * 2, last * 2, tile, 0)

    def add_rows(dst, terms, n):
        def body(i, carry):
            total = terms[0][i].astype(F32)
            for term in terms[1:]:
                total = total + term[i].astype(F32)
            dst[i] = total.astype(dst.dtype)
            return carry
        lax.fori_loop(0, n, body, 0)

    class Ring:
        def __init__(self, axis, chunk, long_buf, short_buf, rows):
            self.axis, self.chunk, self.long_buf, self.short_buf, self.rows = axis, chunk, long_buf, short_buf, rows
            self.n = AXES[axis]
            self.long, self.short = {}, {}

        def _send(self, copies, buf, way, step, dist, half):
            n = self.n
            chunk = self.chunk(dist if way == 0 else n - dist, half)
            if step > 0:
                copies[way, step - 1].arrive()
                add_rows(chunk, [chunk, buf.at[way, step - 1]], self.rows)
            copies[way, step] = push(chunk, buf.at[way, step], ahead[self.axis, 1 if way == 0 else n - 1])

        def send_long(self, way, step):
            self._send(self.long, self.long_buf, way, step, self.n // 2 - step, way)

        def send_short(self, way, step):
            self._send(self.short, self.short_buf, way, step, self.n // 2 - 1 - step, 1 - way)

        def total(self, dst):
            n = self.n
            for way in range(2):
                self.short[way, n // 2 - 2].arrive()
                self.long[way, n // 2 - 1].arrive()
            for half in range(2):
                add_rows(dst(half), [
                    self.chunk(0, half),
                    self.long_buf.at[half, n // 2 - 1],
                    self.short_buf.at[1 - half, n // 2 - 2],
                ], self.rows)

    def spread(axis, src, dst, order):
        return {r: push(src(r), dst(r), ahead[axis, r]) for r in order}

    def settle(copies):
        for copy in copies.values():
            copy.arrive()

    ring_x = [Ring("x", lambda r, h, q=q: PX.at[r, q, pl.ds(2 * h, 2)], RXL.at[q], RXS.at[q], 2) for q in range(Q)]
    ring_y = [Ring("y", lambda r, h, q=q: PY.at[r, q, pl.ds(2 * h, 2)], RYL.at[q], RYS.at[q], 2) for q in range(Q)]
    ring_z = Ring("z", lambda r, h: PZ.at[PLACE[r], pl.ds(2 * h, 2)], RZL, RZS, 2)

    second_x, second_y, third_x, third_y = {}, {}, {}, {}

    def first_hops(q):
        for way in range(2):
            ring_x[q].send_long(way, 0)
            ring_y[q].send_long(way, 0)
        for way in range(2):
            ring_x[q].send_short(way, 0)
            ring_y[q].send_short(way, 0)

    def last_hops(q):
        for way in range(2):
            ring_x[q].send_long(way, 1)
            ring_y[q].send_long(way, 1)

    def second(q):
        ring_x[q].total(lambda half: S2X.at[q, pl.ds(2 * half, 2)])
        second_x[q] = spread("y", lambda r: S2X.at[q, r], lambda r: R2X.at[q, r - 1], (2, 1, 3))
        ring_y[q].total(lambda half: S2Y.at[q, pl.ds(2 * half, 2)])
        second_y[q] = spread("x", lambda r: S2Y.at[q, r], lambda r: R2Y.at[q, r - 1], (2, 1, 3))

    def third(q):
        order = [r for r in ORDER[K * q:K * q + K] if r > 0]
        settle(second_x[q])
        add_rows(S3X.at[pl.ds(K * q, K)], [S2X.at[q, 0]] + [R2X.at[q, r] for r in range(3)], K)
        third_x.update(spread("z", lambda r: S3X.at[PLACE[r]], lambda r: R3X.at[r - 1], order))
        settle(second_y[q])
        add_rows(S3Y.at[pl.ds(K * q, K)], [S2Y.at[q, 0]] + [R2Y.at[q, r] for r in range(3)], K)
        third_y.update(spread("z", lambda r: S3Y.at[PLACE[r]], lambda r: R3Y.at[r - 1], order))

    def z_long(step):
        for way in range(2):
            ring_z.send_long(way, step)

    def z_short(step):
        for way in range(2):
            ring_z.send_short(way, step)

    c_own.wait()
    c_mate.arrive()
    gemm(0, 1)
    z_long(0)
    gemm(1, 2)
    first_hops(0)
    gemm(2, 3)
    z_short(0)
    gemm(3, 4)
    first_hops(1)
    z_long(1)
    gemm(4, 6)
    first_hops(2)
    last_hops(0)
    z_short(1)
    z_long(2)
    gemm(6, 8)
    first_hops(3)
    last_hops(1)
    second(0)
    z_short(2)
    z_long(3)
    last_hops(2)
    second(1)
    third(0)
    last_hops(3)
    second(2)
    third(1)
    ring_z.total(lambda half: S2Z.at[pl.ds(2 * half, 2)])
    second_z = spread("x", lambda r: S2Z.at[r], lambda r: R2Z.at[r - 1], (2, 1, 3))
    second(3)
    third(2)
    settle(second_z)
    add_rows(S3Z, [S2Z.at[0], R2Z.at[0], R2Z.at[1], R2Z.at[2]], 4)
    third_z = spread("y", lambda r: S3Z.at[r], lambda r: R3Z.at[r - 1], (2, 1, 3))
    third(3)

    m_own.wait()
    f_own.wait()
    s_own.wait()

    def adam(gradient, master, first, second):
        new_first = beta_first * first + (1.0 - beta_first) * gradient
        new_second = beta_second * second + (1.0 - beta_second) * gradient * gradient
        first_hat = new_first / (1.0 - beta_first**STEP)
        second_hat = new_second / (1.0 - beta_second**STEP)
        new_master = master - learn_rate * first_hat / (jnp.sqrt(second_hat) + epsilon)
        return new_master, new_first, new_second

    y_hi = y // 2
    own_row = core * 256 + x * 64 + y_hi * 32

    def own_update(stream, own, received, n, dst):
        for i, (row, col) in enumerate(STREAM_UNITS[stream]):
            gradient = own[i].astype(F32)
            for s in range(n):
                gradient = gradient + received[s, i].astype(F32)
            gradient = gradient.astype(BF16)
            GB[0, 0, 0, row * 16:row * 16 + 16, col * 128:col * 128 + 128] = gradient
            rows = pl.ds(pl.multiple_of(own_row + row * 16, 16), 16)
            cols = slice(col * 128, col * 128 + 128)
            new_master, _, _ = adam(gradient.astype(F32), MB[rows, cols], FB[rows, cols], SB[rows, cols])
            dst[i] = new_master.astype(BF16)

    def slot(k):
        return k // K, k % K

    def w_x(k):
        q, kk = slot(k)
        return WX.at[0, q, 0, kk]

    def w_y(k):
        q, kk = slot(k)
        return WY.at[0, q, 0, kk]

    near_first = (1, 7, 2, 6, 3, 5, 4)
    settle(third_z)
    own_update("z", S3Z.at[0], R3Z, 3, WZ.at[7, 0, 0])
    wz1 = spread("y", lambda r: WZ.at[7, 0, 0], lambda r: WZ.at[7, 0, NY - r], (2, 1, 3))
    settle(third_x)
    own_update("x", S3X.at[7], R3X, 7, w_x(7))
    wx1 = spread("z", lambda r: w_x(7), lambda r: w_x(PLACE[NZ - r]), near_first)
    settle(third_y)
    own_update("y", S3Y.at[7], R3Y, 7, w_y(7))
    wy1 = spread("z", lambda r: w_y(7), lambda r: w_y(PLACE[NZ - r]), near_first)
    g1 = spread("x", lambda r: GB.at[0, 0, 0], lambda r: GB.at[0, 0, NX - r], (2, 1, 3))

    class Gather:
        def __init__(self, axis, chunk):
            self.axis, self.chunk, self.n = axis, chunk, AXES[axis]
            self.long, self.short = {}, {}

        def _send(self, copies, way, step, half):
            n = self.n
            if step > 0:
                copies[way, step - 1].arrive()
            r = (n - step) % n if way == 0 else step
            land = (n - step - 1) % n if way == 0 else (step + 1) % n
            copies[way, step] = push(
                self.chunk(r, half), self.chunk(land, half), ahead[self.axis, 1 if way == 0 else n - 1])

        def send_long(self, way, step):
            self._send(self.long, way, step, way)

        def send_short(self, way, step):
            self._send(self.short, way, step, 1 - way)

        def finish(self):
            settle(self.short)
            settle(self.long)

    gather_x = [Gather("x", lambda r, h, q=q: WX.at[r, q, pl.ds(2 * h, 2)]) for q in range(Q)]
    gather_y = [Gather("y", lambda r, h, q=q: WY.at[r, q, pl.ds(2 * h, 2)]) for q in range(Q)]
    gather_z = Gather("z", lambda r, h: WZ.at[PLACE[r], pl.ds(2 * h, 2)])

    across_x, across_y = {}, {}

    def across(q):
        near = [NZ - r for r in ORDER[K * q:K * q + K] if r > 0]
        for r in near:
            wx1[r].arrive()
        across_x[q] = spread("y", lambda r: WX.at[0, q, 0], lambda r: WX.at[0, q, NY - r], (2, 1, 3))
        for r in near:
            wy1[r].arrive()
        across_y[q] = spread("x", lambda r: WY.at[0, q, 0], lambda r: WY.at[0, q, NX - r], (2, 1, 3))

    def go_round(q):
        settle(across_x[q])
        for way in range(2):
            gather_x[q].send_long(way, 0)
        settle(across_y[q])
        for way in range(2):
            gather_y[q].send_long(way, 0)
        for way in range(2):
            gather_x[q].send_short(way, 0)
            gather_y[q].send_short(way, 0)

    def go_on(q):
        for way in range(2):
            gather_x[q].send_long(way, 1)
            gather_y[q].send_long(way, 1)

    def z_gather(step):
        for way in range(2):
            gather_z.send_long(way, step)
            if step < 3:
                gather_z.send_short(way, step)

    def moments(cr):
        def body(i, carry):
            yr, xr = i // 4, lax.rem(i, 4)
            side = core if cr == 0 else 1 - core
            row = side * 256 + lax.rem(x + xr, NX) * 64 + lax.rem(y_hi + yr, 2) * 32
            rows = pl.ds(pl.multiple_of(row, 32), 32)
            new_master, new_first, new_second = adam(
                GB[cr, yr, xr].astype(F32), MB[rows, :], FB[rows, :], SB[rows, :])
            o_master[rows, :] = new_master
            o_first[rows, :] = new_first
            o_second[rows, :] = new_second
            return carry
        lax.fori_loop(0, 8, body, 0)

    def values(q):
        gather_x[q].finish()
        gather_y[q].finish()
        for r in ORDER[K * q:K * q + K]:
            for way in range(2):
                dist = NZ - r if way == 0 else r
                for half, copies in ((way, gather_z.long), (1 - way, gather_z.short)):
                    if (way, dist - 1) in copies:
                        copies[way, dist - 1].arrive()

        def body(j, carry):
            kk, y_lo = j // 2, lax.rem(j, 2)
            for g, xr, yr in groups(y_lo):
                def put(unit, w):
                    row, col = unit
                    at = pl.ds(pl.multiple_of(j * 256 + g * 32 + row * 16, 16), 16)
                    WT[at, col * 128:col * 128 + 128] = w
                for i, unit in enumerate(STREAM_UNITS["x"]):
                    put(unit, WX[xr, q, yr, kk, i])
                for i, unit in enumerate(STREAM_UNITS["y"]):
                    put(unit, WY[yr, q, xr, kk, i])
                for i, unit in enumerate(STREAM_UNITS["z"]):
                    put(unit, WZ[K * q + kk, xr, yr, i])
            return carry
        lax.fori_loop(0, 2 * K, body, 0)
        product = jnp.dot(NB[q], WT[...], preferred_element_type=F32)
        if q == Q - 1:
            VO[...] = product
        else:
            VO[...] += product

    settle(wz1)
    wz2 = spread("x", lambda r: WZ.at[7, 0], lambda r: WZ.at[7, NX - r], (2, 1, 3))
    across(3)
    across(2)
    settle(wz2)
    z_gather(0)
    go_round(3)
    across(1)
    go_round(2)
    across(0)
    settle(g1)
    g2 = push(GB.at[0, 0], GB.at[0, 1], ahead["y", 2])
    z_gather(1)
    go_on(3)
    go_round(1)
    go_on(2)
    z_gather(2)
    go_round(0)
    g2.arrive()
    g3 = push(GB.at[0], GB.at[1], mate)
    go_on(1)
    z_gather(3)
    each(16, lambda t: n_load(t).wait())
    each(16, lambda t: n_push(t).wait_recv())
    moments(0)
    values(3)
    go_on(0)
    g3.arrive()
    moments(1)
    values(2)
    values(1)
    values(0)
    VS[...] = VO[pl.ds(128, 128), :]
    v_mate = push(VS, VR, mate)
    v_mate.arrive()
    o_values[...] = (VO[pl.ds(0, 128), :] + VR[...]).astype(BF16)

    for sent in sends:
        sent.copy.wait_send()
    each(16, lambda t: x_push(t).wait_send())
    each(16, lambda t: n_push(t).wait_send())


def place(a, b, c, d, o_a, o_b, o_c, o_d, sem):
    copies = [
        pltpu.make_async_copy(src, dst, sem.at[i])
        for i, (src, dst) in enumerate(((a, o_a), (b, o_b), (c, o_c), (d, o_d)))
    ]
    for copy in copies:
        copy.start()
    for copy in copies:
        copy.wait()


OUTS = (((512, 512), F32), ((512, 512), F32), ((512, 512), F32), ((128, 512), BF16))


def local_step(layer_input, value_cotangent, master_weight, first_moment, second_moment, next_input):
    unit = (16, 128)

    def vm(*shape, dtype=BF16):
        return pltpu.VMEM(shape, dtype)

    half_xy = (2, K, 3) + unit
    half_z = (2, 4, 2) + unit
    scratch = [
        vm(16, 1024, 256), vm(1024, 512), vm(Q, 256, 1024),
        vm(4, Q, 4, K, 3, *unit), vm(4, Q, 4, K, 3, *unit), vm(8, 4, 4, 2, *unit),
        vm(Q, 2, 2, *half_xy), vm(Q, 2, 1, *half_xy),
        vm(Q, 2, 2, *half_xy), vm(Q, 2, 1, *half_xy),
        vm(2, 4, *half_z), vm(2, 3, *half_z),
        vm(Q, 4, K, 3, *unit), vm(Q, 4, K, 3, *unit), vm(4, 4, 2, *unit),
        vm(Q, 3, K, 3, *unit), vm(Q, 3, K, 3, *unit), vm(3, 4, 2, *unit),
        vm(8, 3, *unit), vm(8, 3, *unit), vm(4, 2, *unit),
        vm(7, 3, *unit), vm(7, 3, *unit), vm(3, 2, *unit),
        vm(4, Q, 4, K, 3, *unit), vm(4, Q, 4, K, 3, *unit), vm(8, 4, 4, 2, *unit),
        vm(2, 2, 4, 32, 512),
        vm(512, 512, dtype=F32), vm(512, 512, dtype=F32), vm(512, 512, dtype=F32),
        vm(1024, 512), vm(256, 512, dtype=F32), vm(128, 512, dtype=F32), vm(128, 512, dtype=F32),
        pltpu.SemaphoreType.DMA((4,)), pltpu.SemaphoreType.DMA((SLOTS,)), pltpu.SemaphoreType.DMA((SLOTS,)),
        pltpu.SemaphoreType.DMA((64,)), pltpu.SemaphoreType.DMA((32,)),
    ]
    results = pl.pallas_call(
        kernel,
        out_shape=tuple(pltpu.VMEM(shape, dtype) for shape, dtype in OUTS),
        in_specs=[pl.BlockSpec(memory_space=pl.ANY)] * 6,
        out_specs=(pl.BlockSpec(memory_space=pltpu.VMEM),) * 4,
        scratch_shapes=scratch,
        compiler_params=pltpu.CompilerParams(
            collective_id=0, has_side_effects=True, vmem_limit_bytes=56 * 2**20),
        cost_estimate=pl.CostEstimate(flops=5_400_000_000, bytes_accessed=18_000_000, transcendentals=0),
        name="value_projection_step",
    )(layer_input, value_cotangent, master_weight, first_moment, second_moment, next_input)
    return tuple(pl.pallas_call(
        place,
        out_shape=tuple(jax.ShapeDtypeStruct(shape, dtype) for shape, dtype in OUTS),
        in_specs=[pl.BlockSpec(memory_space=pltpu.VMEM)] * 4,
        out_specs=(pl.BlockSpec(memory_space=pl.ANY),) * 4,
        scratch_shapes=[pltpu.SemaphoreType.DMA((4,))],
        compiler_params=pltpu.CompilerParams(vmem_limit_bytes=2**20),
        name="place_results",
    )(*results))


def solution(mesh):
    in_specs = (
        P(("cuts", "fsdp"), None),
        P(("cuts", "fsdp"), None),
        P("fsdp", None),
        P("fsdp", None),
        P("fsdp", None),
        P(("cuts", "fsdp"), None),
    )
    out_specs = (P("fsdp", None), P("fsdp", None), P("fsdp", None), P(("cuts", "fsdp"), None))
    return jax.shard_map(local_step, mesh=mesh, in_specs=in_specs, out_specs=out_specs, check_vma=False)
```

time: 727 us -> 77.5 us (0.11)
  waiting for transfers between devices: 688 us -> 0 us
  Pallas kernels: 0 us -> 76.8 us
  matrix products: 19.6 us -> 0 us
  between operations: 13.8 us -> 0.64 us
    reduce_scatter x1 -> x0, waiting for transfers between devices: 355 us -> none  [local(): lax.psum_scatter(contract_tokens(layer_input, value_cotangent), 'fsdp', s...]
    all_gather x1 -> x0, waiting for transfers between devices: 184 us -> none  [local(): lax.all_gather(weight, 'fsdp', axis=0, tiled=True)]
    psum x1 -> x0, waiting for transfers between devices: 149 us -> none  [local(): gradient = lax.psum(slice_grad, 'cuts')]
    pallas_call x0 -> x2, Pallas kernels: none -> 76.8 us  [the longest x1 75.1 us: local_step(): pl.pallas_call(kernel, out_shape=tuple((pltpu.VMEM(shape, dtype) for shap...]
    dot_general x2 -> x0, matrix products: 19.6 us -> none  [the longest x1 13.9 us: contract_tokens(): lax.dot_general(source, cotangent, (((0,), (0,)), ((), ())), preferred_el...]
  transfers between devices with their start and end apart: 3 -> 0, of which waited for: 3 -> 0; matrix products, arithmetic and copies ran while one was open for 0% -> 0% of each run, Pallas kernels for 0% -> 0%
where the time goes in v2:
time: 77.5 us; the launch traced here: 77.4 us
  Pallas kernels  76.8 us (99%)
    pallas_call x1, Pallas kernels, local_step(): pl.pallas_call(kernel, out_shape=tuple((pltpu.VMEM(shape, dtype) for shap...  75.1 us
    pallas_call x1, Pallas kernels, local_step(): pl.pallas_call(place, out_shape=tuple((jax.ShapeDtypeStruct(shape, dtype)...  1.73 us

profile of v2, /device:TPU:1, one launch (start us, length us, event | category | flops | bytes accessed | tf_op | source)
XLA Modules:
  0.0 77.4 jit_solution(13305263544420643223)
XLA Ops:
  0.6 75.1 %value_projection_step.1 = (f32[512,512]{1,0:T(8,128)S(1)}, f32[512,512]{1,0:T(8,128)S(1)}, f32[512,512]{1,0:T(8,128)S(1)}, bf16[128,512]{1,0:T(8,128)(2,1)S(1)}) custom-call(bf16[512,8192]{1,0:T(8,128)(2,1)} %x_hbm.1, bf16[512,512]{1,0:T(8,128)(2,1)} %c_hbm.1, f32[512,512]{1,0:T(8,128)} %master_hbm.1, f32[512,512]{1,0:T(8,128)} %first_hbm.1, ...), custom_call_target="tpu_custom_call" | custom-call | flops 5400000000 | bytes 18000000 | tf_op jit(solution)/shard_map/value_projection_step/pallas_call | solution.py:539
  75.7 1.7 %place_results.1 = (f32[512,512]{1,0:T(8,128)}, f32[512,512]{1,0:T(8,128)}, f32[512,512]{1,0:T(8,128)}, bf16[128,512]{1,0:T(8,128)(2,1)}) custom-call(f32[512,512]{1,0:T(8,128)S(1)} %get-tuple-element.8.a, f32[512,512]{1,0:T(8,128)S(1)} %get-tuple-element.9.b, f32[512,512]{1,0:T(8,128)S(1)} %get-tuple-element.10.c, bf16[128,512]{1,0:T(8,128)(2,1)S(1)} %get-tuple-element.11.d), custom_call_target="tpu_custom_call" | custom-call | tf_op jit(solution)/shard_map/place_results/pallas_call | solution.py:550

commit v3 on v0

v3 whole, which is shorter than its diff:
```python
import functools

import jax
import jax.numpy as jnp
from jax import lax
from jax.experimental import pallas as pl
from jax.experimental.pallas import tpu as pltpu
from jax.sharding import PartitionSpec as P

STEP = 200
beta_first = 0.9
beta_second = 0.95
learn_rate = 0.001
epsilon = 1e-08

MESH = pl.DeviceIdType.MESH
BF16 = jnp.bfloat16
F32 = jnp.float32

NX, NY, NZ = 4, 4, 8
POOL = 24
ARRIVALS = 80
AXES = {"x": NX, "y": NY, "z": NZ}
ORDER = (4, 3, 5, 2, 6, 1, 7, 0)
PLACE = {r: k for k, r in enumerate(ORDER)}
Q = 4
K = NZ // Q
PARTS = 4
STREAMS = {
    "x": ("x", "y", [(0, 0), (0, 1), (0, 2)]),
    "y": ("y", "x", [(0, 3), (1, 0), (1, 1)]),
}
Z_UNITS = [(1, 2), (1, 3)]


def position():
    cuts, fsdp = lax.axis_index("cuts"), lax.axis_index("fsdp")
    x, y_hi, core = cuts // 4, lax.rem(cuts // 2, 2), lax.rem(cuts, 2)
    z, y_lo = fsdp // 2, lax.rem(fsdp, 2)
    return x, y_hi * 2 + y_lo, z, core


def device(x, y, z, core):
    return (x * 4 + (y // 2) * 2 + core, z * 2 + lax.rem(y, 2))


def kernel(
    x_hbm, c_hbm, master_hbm, first_hbm, second_hbm, next_hbm,
    o_master, o_first, o_second, o_values,
    XB, CB, NB, PZ, RZL, RZS, S2Z, R2Z, S3Z, R3Z, WZ,
    buf_x, buf_y,
    GB, MFS, WT, VO, VS, VR,
    send_sem, recv_sem, x_sem, bulk_sem,
):
    x, y, z, core = position()
    here = {"x": x, "y": y, "z": z}

    def towards(axis, delta):
        at = dict(here)
        at[axis] = lax.rem(here[axis] + delta, AXES[axis])
        return device(at["x"], at["y"], at["z"], core)

    mate = device(x, y, z, 1 - core)
    ahead = {(a, d): towards(a, d) for a in "xyz" for d in range(1, AXES[a])}

    barrier = pltpu.get_barrier_semaphore()
    partners = [mate] + [ahead[key] for key in sorted(ahead, key=lambda p: -min(p[1], AXES[p[0]] - p[1]))]
    for dev in partners:
        pl.semaphore_signal(barrier, inc=1, device_id=dev, device_id_type=MESH)

    counts = {"arrival": 0, "group": 0}
    pool = [None] * POOL

    def arrival():
        counts["arrival"] += 1
        return recv_sem.at[counts["arrival"] - 1]

    def wait_bytes(ref, sem):
        pltpu.make_async_copy(ref, ref, sem).wait()

    class Group:
        def __init__(self, items, whole, recv=None):
            slot = counts["group"] % POOL
            counts["group"] += 1
            if pool[slot] is not None:
                pool[slot].leave()
            pool[slot] = self
            self.whole, self.sem = whole, send_sem.at[slot]
            self.recv = arrival() if recv is None else None
            self.landed = recv is not None
            for i, (src, dst, dev) in enumerate(items):
                sem = self.recv if recv is None else recv[i] if isinstance(recv, list) else recv
                pltpu.make_async_remote_copy(
                    src_ref=src, dst_ref=dst, send_sem=self.sem, recv_sem=sem,
                    device_id=dev, device_id_type=MESH,
                ).start()

        def leave(self):
            wait_bytes(self.whole, self.sem)

        def arrive(self):
            if not self.landed:
                self.landed = True
                wait_bytes(self.whole, self.recv)

    def block_of(t):
        k = t // 2
        odd = lax.rem(k, 2)
        r = 4 + (1 - odd) * (k // 2) - odd * ((k + 1) // 2)
        return lax.rem(z + r, NZ) * 2 + lax.rem(t, 2)

    def columns(t, side):
        return pl.ds(pl.multiple_of(block_of(t) * 512 + side * 256, 256), 256)

    def x_load(t):
        return pltpu.make_async_copy(
            x_hbm.at[:, columns(t, core)], XB.at[t, pl.ds(0, 512)], x_sem.at[t])

    def x_push(t):
        return pltpu.make_async_remote_copy(
            src_ref=x_hbm.at[:, columns(t, 1 - core)], dst_ref=XB.at[t, pl.ds(512, 512)],
            send_sem=bulk_sem.at[0], recv_sem=x_sem.at[t], device_id=mate, device_id_type=MESH)

    def n_place(t, rows):
        return NB.at[t // 4, pl.ds(rows, 128), pl.ds(pl.multiple_of(lax.rem(t, 4) * 256, 256), 256)]

    def n_load(t):
        return pltpu.make_async_copy(next_hbm.at[:, columns(t, core)], n_place(t, 0), bulk_sem.at[2])

    def n_push(t):
        return pltpu.make_async_remote_copy(
            src_ref=next_hbm.at[:, columns(t, 1 - core)], dst_ref=n_place(t, 128),
            send_sem=bulk_sem.at[1], recv_sem=bulk_sem.at[2], device_id=mate, device_id_type=MESH)

    def each(n, act):
        def body(t, carry):
            act(t)
            return carry
        lax.fori_loop(0, n, body, 0)

    c_sem = arrival()
    pltpu.make_async_copy(c_hbm, CB.at[pl.ds(0, 512)], c_sem).start()
    each(16, lambda t: x_load(t).start())
    pl.semaphore_wait(barrier, len(partners))

    Group([(c_hbm, CB.at[pl.ds(512, 512)], mate)], CB.at[pl.ds(512, 512)], c_sem)
    each(16, lambda t: x_push(t).start())
    for i, ref in enumerate((master_hbm, first_hbm, second_hbm)):
        pltpu.make_async_copy(ref, MFS.at[i], bulk_sem.at[3]).start()
    each(16, lambda t: n_load(t).start())
    each(16, lambda t: n_push(t).start())

    def groups(y_lo):
        out = []
        for g in range(8):
            xr = lax.rem(g // 2 + NX - x, NX)
            yr = lax.rem((g % 2) * 2 + y_lo + NY - y, NY)
            out.append((g, xr, yr))
        return out

    def tile(t, carry):
        wait_bytes(XB.at[t], x_sem.at[t])
        g_tile = lax.dot_general(
            XB[t], CB[...], (((0,), (0,)), ((), ())), preferred_element_type=F32).astype(BF16)
        k, y_lo = t // 2, lax.rem(t, 2)
        q, kk = k // K, lax.rem(k, K)

        def piece(g, unit):
            row, col = unit
            return g_tile[g * 32 + row * 16:g * 32 + row * 16 + 16, col * 128:col * 128 + 128]

        for g, xr, yr in groups(y_lo):
            for st in streams.values():
                for i, unit in enumerate(st.units):
                    st.P[st.places(xr, q, yr, kk, i)] = piece(g, unit)
            for i, unit in enumerate(Z_UNITS):
                PZ[k, xr, yr, i] = piece(g, unit)
        return carry

    def gemm(first, last):
        lax.fori_loop(first * 2, last * 2, tile, 0)

    def add_rows(dst, terms, n):
        def body(i, carry):
            total = terms[0][i].astype(F32)
            for term in terms[1:]:
                total = total + term[i].astype(F32)
            dst[i] = total.astype(dst.dtype)
            return carry
        lax.fori_loop(0, n, body, 0)

    def both_ways(axis):
        return ahead[axis, 1], ahead[axis, AXES[axis] - 1]

    class Ring:
        def __init__(self, axis, chunk, long_buf, short_buf, rows):
            self.axis, self.chunk, self.long_buf, self.short_buf, self.rows = axis, chunk, long_buf, short_buf, rows
            self.n = AXES[axis]
            self.long, self.short, self.last = {}, {}, None

        def _send(self, copies, buf, step, dist, halves, recv=None):
            chunks = [self.chunk(dist, halves[0]), self.chunk(self.n - dist, halves[1])]
            if step > 0:
                copies[step - 1].arrive()
                for way in range(2):
                    add_rows(chunks[way], [chunks[way], buf.at[step - 1, way]], self.rows)
            devs = both_ways(self.axis)
            copies[step] = Group([(chunks[w], buf.at[step, w], devs[w]) for w in range(2)], buf.at[step], recv)

        def send_long(self, step, recv=None):
            self._send(self.long, self.long_buf, step, self.n // 2 - step, (0, 1), recv)

        def send_short(self, step, recv=None):
            self._send(self.short, self.short_buf, step, self.n // 2 - 1 - step, (1, 0), recv)

        def total(self, dst):
            n = self.n
            for half in range(2):
                add_rows(dst(half), [
                    self.chunk(0, half),
                    self.long_buf.at[n // 2 - 1, half],
                    self.short_buf.at[n // 2 - 2, 1 - half],
                ], self.rows)

    def spread(axis, src, dst, order, whole, recv=None):
        return Group([(src(r), dst(r), ahead[axis, r]) for r in order], whole, recv)

    ring_z = Ring("z", lambda r, h: PZ.at[PLACE[r], pl.ds(2 * h, 2)], RZL, RZS, 2)

    def z_long(step):
        ring_z.send_long(step)

    def z_short(step):
        ring_z.send_short(step)

    def adam(gradient, master, first, second):
        new_first = beta_first * first + (1.0 - beta_first) * gradient
        new_second = beta_second * second + (1.0 - beta_second) * gradient * gradient
        first_hat = new_first / (1.0 - beta_first**STEP)
        second_hat = new_second / (1.0 - beta_second**STEP)
        new_master = master - learn_rate * first_hat / (jnp.sqrt(second_hat) + epsilon)
        return new_master, new_first, new_second

    y_hi = y // 2
    own_row = core * 256 + x * 64 + y_hi * 32

    def own_update(units, own, received, n, dst):
        for n_unit, (row, col) in enumerate(units):
            gradient = own[n_unit].astype(F32)
            for s in range(n):
                gradient = gradient + received[s, n_unit].astype(F32)
            gradient = gradient.astype(BF16)
            GB[0, 0, 0, row * 16:row * 16 + 16, col * 128:col * 128 + 128] = gradient
            rows = pl.ds(pl.multiple_of(own_row + row * 16, 16), 16)
            cols = slice(col * 128, col * 128 + 128)
            new_master, _, _ = adam(gradient.astype(F32), *(MFS[i, rows, cols] for i in range(3)))
            dst[n_unit] = new_master.astype(BF16)

    near_first = (1, 7, 2, 6, 3, 5, 4)

    class Stream:
        def __init__(self, name, bufs):
            self.axis, self.other, self.units = STREAMS[name]
            self.P, self.RL, self.RS, self.S2, self.R2, self.S3, self.R3, self.W = bufs
            self.two, self.near, self.across_, self.long = {}, {}, {}, {}
            self.ring_last = [arrival() for _ in range(Q)]
            self.gather_last = [arrival() for _ in range(Q)]
            self.back = [arrival() for _ in range(Q)]
            self.three = arrival()

        def half(self, r, q, h):
            return self.P.at[r, q, pl.ds(2 * h, 2)]

        def part(self, r, q, h):
            return self.W.at[r, q, pl.ds(2 * h, 2)]

        def places(self, xr, q, yr, kk, i):
            return (xr, q, yr, kk, i) if self.axis == "x" else (yr, q, xr, kk, i)

        def hop0(self, q):
            devs = both_ways(self.axis)
            self.near[q] = Group(
                [(self.half(2, q, w), self.RL.at[q, w], devs[w]) for w in range(2)], self.RL.at[q])
            Group(
                [(self.half(1 + 2 * w, q, 1 - w), self.RS.at[q, 2 + w], devs[w]) for w in range(2)],
                self.RL.at[q], self.ring_last[q])

        def hop1(self, q):
            devs = both_ways(self.axis)
            self.near[q].arrive()
            for w in range(2):
                chunk = self.half(1 + 2 * w, q, w)
                add_rows(chunk, [chunk, self.RL.at[q, w]], 2)
            Group(
                [(self.half(1 + 2 * w, q, w), self.RS.at[q, w], devs[w]) for w in range(2)],
                self.RL.at[q], self.ring_last[q])

        def second(self, q):
            wait_bytes(self.RS.at[q], self.ring_last[q])
            for h in range(2):
                add_rows(
                    self.S2.at[q, pl.ds(2 * h, 2)], [self.half(0, q, h), self.RS.at[q, h], self.RS.at[q, 3 - h]], 2)
            self.two[q] = spread(
                self.other, lambda r: self.S2.at[q, r], lambda r: self.R2.at[q, r - 1], (2, 1, 3), self.R2.at[q])

        def third(self, q):
            self.two[q].arrive()
            add_rows(self.S3.at[pl.ds(K * q, K)], [self.S2.at[q, 0]] + [self.R2.at[q, r] for r in range(3)], K)
            order = [r for r in ORDER[K * q:K * q + K] if r > 0]
            spread("z", lambda r: self.S3.at[PLACE[r]], lambda r: self.R3.at[r - 1], order,
                   self.S3.at[pl.ds(K * q, len(order))], self.three)

        def own(self, r):
            return self.W.at[0, PLACE[r] // K, 0, PLACE[r] % K]

        def update(self):
            wait_bytes(self.R3, self.three)
            own_update(self.units, self.S3.at[7], self.R3, 7, self.own(0))
            spread("z", lambda r: self.own(0), lambda r: self.own(NZ - r), near_first, self.R3,
                   [self.back[PLACE[NZ - r] // K] for r in near_first])

        def across(self, q):
            came = len([r for r in ORDER[K * q:K * q + K] if r > 0])
            wait_bytes(self.W.at[0, q, 0, pl.ds(0, came)], self.back[q])
            self.across_[q] = spread(
                self.other, lambda r: self.W.at[0, q, 0], lambda r: self.W.at[0, q, 4 - r], (2, 1, 3),
                self.W.at[0, q, pl.ds(1, 3)])

        def go0(self, q):
            devs = both_ways(self.axis)
            self.across_[q].arrive()
            self.long[q] = Group(
                [(self.part(0, q, w), self.part(3 - 2 * w, q, w), devs[w]) for w in range(2)], self.W.at[0, q])
            Group(
                [(self.part(0, q, 1 - w), self.part(3 - 2 * w, q, 1 - w), devs[w]) for w in range(2)],
                self.W.at[0, q], self.gather_last[q])

        def go1(self, q):
            devs = both_ways(self.axis)
            self.long[q].arrive()
            Group(
                [(self.part(3 - 2 * w, q, w), self.part(2, q, w), devs[w]) for w in range(2)],
                self.W.at[0, q], self.gather_last[q])

        def finish(self, q):
            wait_bytes(self.W.at[pl.ds(0, 2), q], self.gather_last[q])

    streams = {name: Stream(name, bufs) for name, bufs in zip(STREAMS, (buf_x, buf_y))}
    x_s, y_s = streams.values()
    zs = {}

    def z_second():
        ring_z.long[3].arrive()
        ring_z.short[2].arrive()
        ring_z.total(lambda half: S2Z.at[pl.ds(2 * half, 2)])
        zs["two"] = spread("x", lambda r: S2Z.at[r], lambda r: R2Z.at[r - 1], (2, 1, 3), R2Z)

    def z_third():
        zs["two"].arrive()
        add_rows(S3Z, [S2Z.at[0], R2Z.at[0], R2Z.at[1], R2Z.at[2]], 4)
        zs["three"] = spread("y", lambda r: S3Z.at[r], lambda r: R3Z.at[r - 1], (2, 1, 3), R3Z)

    def z_update():
        zs["three"].arrive()
        own_update(Z_UNITS, S3Z.at[0], R3Z, 3, WZ.at[7, 0, 0])
        zs["back_y"] = spread(
            "y", lambda r: WZ.at[7, 0, 0], lambda r: WZ.at[7, 0, NY - r], (2, 1, 3), WZ.at[7, 0, pl.ds(1, 3)])

    def z_across():
        zs["back_y"].arrive()
        zs["back_x"] = spread(
            "x", lambda r: WZ.at[7, 0], lambda r: WZ.at[7, NX - r], (2, 1, 3), WZ.at[7, pl.ds(1, 3)])

    def z_gather(step):
        if step == 0:
            zs["back_x"].arrive()
        else:
            zs["gather", step - 1].arrive()
        devs = both_ways("z")
        items = []
        for way in range(2):
            r = (NZ - step) % NZ if way == 0 else step
            land = NZ - step - 1 if way == 0 else step + 1
            for half in ((0, 1) if step < 3 else (way,)):
                rows = pl.ds(2 * half, 2)
                items.append((WZ.at[PLACE[r], rows], WZ.at[PLACE[land], rows], devs[way]))
        zs["gather", step] = Group(items, WZ.at[pl.ds(0, 2)] if step < 3 else WZ.at[0])

    def states():
        wait_bytes(MFS, bulk_sem.at[3])

    def rows_1():
        zs["g1"] = spread(
            "x", lambda r: GB.at[0, 0, 0], lambda r: GB.at[0, 0, NX - r], (2, 1, 3), GB.at[0, 0, pl.ds(1, 3)])

    def rows_2():
        zs["g1"].arrive()
        zs["g2"] = Group([(GB.at[0, 0], GB.at[0, 1], ahead["y", 2])], GB.at[0, 0])

    def rows_3():
        zs["g2"].arrive()
        zs["g3"] = Group([(GB.at[0], GB.at[1], mate)], GB.at[0])

    def moments(cr):
        def body(i, carry):
            yr, xr = i // 4, lax.rem(i, 4)
            side = core if cr == 0 else 1 - core
            row = side * 256 + lax.rem(x + xr, NX) * 64 + lax.rem(y_hi + yr, 2) * 32
            rows = pl.ds(pl.multiple_of(row, 32), 32)
            new_master, new_first, new_second = adam(
                GB[cr, yr, xr].astype(F32), *(MFS[j, rows, :] for j in range(3)))
            o_master[rows, :] = new_master
            o_first[rows, :] = new_first
            o_second[rows, :] = new_second
            return carry
        lax.fori_loop(0, 8, body, 0)

    def values(part):
        blocks = NZ // PARTS
        first = part * blocks
        for st in streams.values():
            for q in sorted({(first + i) // K for i in range(blocks)}):
                st.finish(q)
        for step in range(max(min(r, NZ - r) for r in ORDER[first:first + blocks])):
            zs["gather", step].arrive()

        def body(j, carry):
            y_lo = lax.rem(j, 2)
            k = first + j // 2
            q, kk = k // K, lax.rem(k, K)
            for g, xr, yr in groups(y_lo):
                def put(unit, w):
                    row, col = unit
                    at = pl.ds(pl.multiple_of(j * 256 + g * 32 + row * 16, 16), 16)
                    WT[at, col * 128:col * 128 + 128] = w
                for st in streams.values():
                    for i, unit in enumerate(st.units):
                        put(unit, st.W[st.places(xr, q, yr, kk, i)])
                for i, unit in enumerate(Z_UNITS):
                    put(unit, WZ[k, xr, yr, i])
            return carry
        lax.fori_loop(0, 2 * blocks, body, 0)
        product = jnp.dot(NB[part], WT[...], preferred_element_type=F32)
        if part == PARTS - 1:
            VO[...] = product
        else:
            VO[...] += product

    def nexts():
        wait_bytes(NB, bulk_sem.at[2])

    v_sem = arrival()

    def last_swap():
        VS[...] = VO[pl.ds(128, 128), :]
        Group([(VS, VR, mate)], VR, v_sem)
        wait_bytes(VR, v_sem)
        o_values[...] = (VO[pl.ds(0, 128), :] + VR[...]).astype(BF16)

    wait_bytes(CB, c_sem)
    gemm(0, 1)
    z_long(0)
    gemm(1, 2)
    x_s.hop0(0)
    y_s.hop0(0)
    gemm(2, 3)
    z_short(0)
    gemm(3, 4)
    states()
    x_s.hop0(1)
    y_s.hop0(1)
    gemm(4, 5)
    z_long(1)
    x_s.hop1(0)
    y_s.hop1(0)
    gemm(5, 6)
    y_s.hop0(2)
    x_s.hop0(2)
    z_short(1)
    x_s.hop1(1)
    gemm(6, 7)
    y_s.hop1(1)
    z_long(2)
    gemm(7, 8)
    x_s.hop0(3)
    x_s.second(0)
    y_s.hop0(3)
    z_short(2)
    x_s.hop1(2)
    z_long(3)
    y_s.hop1(2)
    y_s.second(1)
    x_s.hop1(3)
    x_s.second(1)
    x_s.third(0)
    y_s.second(0)
    y_s.hop1(3)
    nexts()
    x_s.second(2)
    z_second()
    y_s.third(1)
    y_s.second(2)
    x_s.second(3)
    x_s.third(1)
    y_s.second(3)
    y_s.third(0)
    x_s.third(2)
    z_third()
    x_s.third(3)
    y_s.third(2)
    y_s.third(3)
    z_update()
    x_s.update()
    y_s.update()
    rows_1()
    x_s.across(3)
    z_across()
    x_s.across(2)
    y_s.across(3)
    rows_2()
    x_s.across(1)
    y_s.across(2)
    x_s.go0(3)
    x_s.across(0)
    z_gather(0)
    y_s.across(1)
    y_s.go0(3)
    y_s.across(0)
    x_s.go0(2)
    y_s.go0(2)
    z_gather(1)
    y_s.go0(1)
    rows_3()
    x_s.go0(1)
    x_s.go1(3)
    x_s.go1(2)
    x_s.go0(0)
    y_s.go1(3)
    y_s.go0(0)
    z_gather(2)
    moments(0)
    x_s.go1(1)
    y_s.go1(2)
    y_s.go1(1)
    zs["g3"].arrive()
    moments(1)
    values(3)
    y_s.go1(0)
    z_gather(3)
    x_s.go1(0)
    values(2)
    values(1)
    values(0)
    last_swap()
    for group in pool:
        if group is not None:
            group.leave()
    wait_bytes(XB.at[pl.ds(0, 8)], bulk_sem.at[0])
    wait_bytes(NB.at[pl.ds(0, 2)], bulk_sem.at[1])


def place(a, b, c, d, o_a, o_b, o_c, o_d, sem):
    copies = [
        pltpu.make_async_copy(src, dst, sem.at[i])
        for i, (src, dst) in enumerate(((a, o_a), (b, o_b), (c, o_c), (d, o_d)))
    ]
    for copy in copies:
        copy.start()
    for copy in copies:
        copy.wait()


OUTS = (((512, 512), F32), ((512, 512), F32), ((512, 512), F32), ((128, 512), BF16))


def local_step(layer_input, value_cotangent, master_weight, first_moment, second_moment, next_input):
    unit = (16, 128)

    def vm(*shape, dtype=BF16):
        return pltpu.VMEM(shape, dtype)

    def stream_buffers(n):
        u = (n,) + unit
        return (
            vm(4, Q, 4, K, *u), vm(Q, 2, 2, K, *u), vm(Q, 4, 2, K, *u), vm(Q, 4, K, *u), vm(Q, 3, K, *u),
            vm(8, *u), vm(7, *u), vm(4, Q, 4, K, *u))

    half_z = (2, 4, 2) + unit
    scratch = [
        vm(16, 1024, 256), vm(1024, 512), vm(4, 256, 1024),
        vm(8, 4, 4, 2, *unit), vm(4, 2, *half_z), vm(3, 2, *half_z),
        vm(4, 4, 2, *unit), vm(3, 4, 2, *unit), vm(4, 2, *unit), vm(3, 2, *unit), vm(8, 4, 4, 2, *unit),
        *[stream_buffers(len(STREAMS[name][2])) for name in STREAMS],
        vm(2, 2, 4, 32, 512),
        vm(3, 512, 512, dtype=F32),
        vm(1024, 512), vm(256, 512, dtype=F32), vm(128, 512, dtype=F32), vm(128, 512, dtype=F32),
        pltpu.SemaphoreType.DMA((POOL,)), pltpu.SemaphoreType.DMA((ARRIVALS,)),
        pltpu.SemaphoreType.DMA((16,)), pltpu.SemaphoreType.DMA((4,)),
    ]
    results = pl.pallas_call(
        kernel,
        out_shape=tuple(pltpu.VMEM(shape, dtype) for shape, dtype in OUTS),
        in_specs=[pl.BlockSpec(memory_space=pl.ANY)] * 6,
        out_specs=(pl.BlockSpec(memory_space=pltpu.VMEM),) * 4,
        scratch_shapes=scratch,
        compiler_params=pltpu.CompilerParams(
            collective_id=0, has_side_effects=True, vmem_limit_bytes=56 * 2**20),
        cost_estimate=pl.CostEstimate(flops=5_400_000_000, bytes_accessed=18_000_000, transcendentals=0),
        name="value_projection_step",
    )(layer_input, value_cotangent, master_weight, first_moment, second_moment, next_input)
    return tuple(pl.pallas_call(
        place,
        out_shape=tuple(jax.ShapeDtypeStruct(shape, dtype) for shape, dtype in OUTS),
        in_specs=[pl.BlockSpec(memory_space=pltpu.VMEM)] * 4,
        out_specs=(pl.BlockSpec(memory_space=pl.ANY),) * 4,
        scratch_shapes=[pltpu.SemaphoreType.DMA((4,))],
        compiler_params=pltpu.CompilerParams(vmem_limit_bytes=2**20),
        name="place_results",
    )(*results))


def solution(mesh):
    in_specs = (
        P(("cuts", "fsdp"), None),
        P(("cuts", "fsdp"), None),
        P("fsdp", None),
        P("fsdp", None),
        P("fsdp", None),
        P(("cuts", "fsdp"), None),
    )
    out_specs = (P("fsdp", None), P("fsdp", None), P("fsdp", None), P(("cuts", "fsdp"), None))
    return jax.shard_map(local_step, mesh=mesh, in_specs=in_specs, out_specs=out_specs, check_vma=False)
```

time: 727 us -> 71.3 us (0.10)
  waiting for transfers between devices: 688 us -> 0 us
  Pallas kernels: 0 us -> 70.6 us
  matrix products: 19.6 us -> 0 us
  between operations: 13.8 us -> 0.64 us
    reduce_scatter x1 -> x0, waiting for transfers between devices: 355 us -> none  [local(): lax.psum_scatter(contract_tokens(layer_input, value_cotangent), 'fsdp', s...]
    all_gather x1 -> x0, waiting for transfers between devices: 184 us -> none  [local(): lax.all_gather(weight, 'fsdp', axis=0, tiled=True)]
    psum x1 -> x0, waiting for transfers between devices: 149 us -> none  [local(): gradient = lax.psum(slice_grad, 'cuts')]
    pallas_call x0 -> x2, Pallas kernels: none -> 70.6 us  [the longest x1 68.9 us: local_step(): pl.pallas_call(kernel, out_shape=tuple((pltpu.VMEM(shape, dtype) for shap...]
    dot_general x2 -> x0, matrix products: 19.6 us -> none  [the longest x1 13.9 us: contract_tokens(): lax.dot_general(source, cotangent, (((0,), (0,)), ((), ())), preferred_el...]
  transfers between devices with their start and end apart: 3 -> 0, of which waited for: 3 -> 0; matrix products, arithmetic and copies ran while one was open for 0% -> 0% of each run, Pallas kernels for 0% -> 0%
where the time goes in v3:
time: 71.3 us; the launch traced here: 71.2 us
  Pallas kernels  70.6 us (99%)
    pallas_call x1, Pallas kernels, local_step(): pl.pallas_call(kernel, out_shape=tuple((pltpu.VMEM(shape, dtype) for shap...  68.9 us
    pallas_call x1, Pallas kernels, local_step(): pl.pallas_call(place, out_shape=tuple((jax.ShapeDtypeStruct(shape, dtype)...  1.73 us

profile of v3, /device:TPU:1, one launch (start us, length us, event | category | flops | bytes accessed | tf_op | source)
XLA Modules:
  0.0 71.2 jit_solution(17118017473838863335)
XLA Ops:
  0.6 68.9 %value_projection_step.1 = (f32[512,512]{1,0:T(8,128)S(1)}, f32[512,512]{1,0:T(8,128)S(1)}, f32[512,512]{1,0:T(8,128)S(1)}, bf16[128,512]{1,0:T(8,128)(2,1)S(1)}) custom-call(bf16[512,8192]{1,0:T(8,128)(2,1)} %x_hbm.1, bf16[512,512]{1,0:T(8,128)(2,1)} %c_hbm.1, f32[512,512]{1,0:T(8,128)} %master_hbm.1, f32[512,512]{1,0:T(8,128)} %first_hbm.1, ...), custom_call_target="tpu_custom_call" | custom-call | flops 5400000000 | bytes 18000000 | tf_op jit(solution)/shard_map/value_projection_step/pallas_call | solution.py:600
  69.5 1.7 %place_results.1 = (f32[512,512]{1,0:T(8,128)}, f32[512,512]{1,0:T(8,128)}, f32[512,512]{1,0:T(8,128)}, bf16[128,512]{1,0:T(8,128)(2,1)}) custom-call(f32[512,512]{1,0:T(8,128)S(1)} %get-tuple-element.8.a, f32[512,512]{1,0:T(8,128)S(1)} %get-tuple-element.9.b, f32[512,512]{1,0:T(8,128)S(1)} %get-tuple-element.10.c, bf16[128,512]{1,0:T(8,128)(2,1)S(1)} %get-tuple-element.11.d), custom_call_target="tpu_custom_call" | custom-call | tf_op jit(solution)/shard_map/place_results/pallas_call | solution.py:611

commit v4 on v3

--- a/solution.py
+++ b/solution.py
@@ -23,9 +23,10 @@
 AXES = {"x": NX, "y": NY, "z": NZ}
 ORDER = (4, 3, 5, 2, 6, 1, 7, 0)
 PLACE = {r: k for k, r in enumerate(ORDER)}
-Q = 4
-K = NZ // Q
-PARTS = 4
+GROUPS = (1, 2, 2, 3)
+START = tuple(sum(GROUPS[:q]) for q in range(len(GROUPS)))
+GROUP = tuple(q for q, size in enumerate(GROUPS) for _ in range(size))
+Q = len(GROUPS)
 STREAMS = {
     "x": ("x", "y", [(0, 0), (0, 1), (0, 2)]),
     "y": ("y", "x", [(0, 3), (1, 0), (1, 1)]),
@@ -49,7 +50,7 @@
     o_master, o_first, o_second, o_values,
     XB, CB, NB, PZ, RZL, RZS, S2Z, R2Z, S3Z, R3Z, WZ,
     buf_x, buf_y,
-    GB, MFS, WT, VO, VS, VR,
+    GB, MFS, WT, VO, VR,
     send_sem, recv_sem, x_sem, bulk_sem,
 ):
     x, y, z, core = position()
@@ -122,7 +123,7 @@
             send_sem=bulk_sem.at[0], recv_sem=x_sem.at[t], device_id=mate, device_id_type=MESH)
 
     def n_place(t, rows):
-        return NB.at[t // 4, pl.ds(rows, 128), pl.ds(pl.multiple_of(lax.rem(t, 4) * 256, 256), 256)]
+        return NB.at[pl.ds(rows, 128), pl.ds(pl.multiple_of(t * 256, 256), 256)]
 
     def n_load(t):
         return pltpu.make_async_copy(next_hbm.at[:, columns(t, core)], n_place(t, 0), bulk_sem.at[2])
@@ -158,12 +159,12 @@
             out.append((g, xr, yr))
         return out
 
-    def tile(t, carry):
+    def tile(k, y_lo, carry):
+        t = 2 * k + y_lo
         wait_bytes(XB.at[t], x_sem.at[t])
         g_tile = lax.dot_general(
             XB[t], CB[...], (((0,), (0,)), ((), ())), preferred_element_type=F32).astype(BF16)
-        k, y_lo = t // 2, lax.rem(t, 2)
-        q, kk = k // K, lax.rem(k, K)
+        q, kk = GROUP[k], k - START[GROUP[k]]
 
         def piece(g, unit):
             row, col = unit
@@ -172,13 +173,14 @@
         for g, xr, yr in groups(y_lo):
             for st in streams.values():
                 for i, unit in enumerate(st.units):
-                    st.P[st.places(xr, q, yr, kk, i)] = piece(g, unit)
+                    st.P[q][st.places(xr, yr, kk, i)] = piece(g, unit)
             for i, unit in enumerate(Z_UNITS):
                 PZ[k, xr, yr, i] = piece(g, unit)
         return carry
 
     def gemm(first, last):
-        lax.fori_loop(first * 2, last * 2, tile, 0)
+        for k in range(first, last):
+            lax.fori_loop(0, 2, functools.partial(tile, k), 0)
 
     def add_rows(dst, terms, n):
         def body(i, carry):
@@ -267,83 +269,86 @@
             self.gather_last = [arrival() for _ in range(Q)]
             self.back = [arrival() for _ in range(Q)]
             self.three = arrival()
+            self.done = set()
 
         def half(self, r, q, h):
-            return self.P.at[r, q, pl.ds(2 * h, 2)]
+            return self.P[q].at[r, pl.ds(2 * h, 2)]
 
         def part(self, r, q, h):
-            return self.W.at[r, q, pl.ds(2 * h, 2)]
-
-        def places(self, xr, q, yr, kk, i):
-            return (xr, q, yr, kk, i) if self.axis == "x" else (yr, q, xr, kk, i)
+            return self.W[q].at[r, pl.ds(2 * h, 2)]
+
+        def places(self, xr, yr, kk, i):
+            return (xr, yr, kk, i) if self.axis == "x" else (yr, xr, kk, i)
 
         def hop0(self, q):
             devs = both_ways(self.axis)
             self.near[q] = Group(
-                [(self.half(2, q, w), self.RL.at[q, w], devs[w]) for w in range(2)], self.RL.at[q])
+                [(self.half(2, q, w), self.RL[q].at[w], devs[w]) for w in range(2)], self.RL[q])
             Group(
-                [(self.half(1 + 2 * w, q, 1 - w), self.RS.at[q, 2 + w], devs[w]) for w in range(2)],
-                self.RL.at[q], self.ring_last[q])
+                [(self.half(1 + 2 * w, q, 1 - w), self.RS[q].at[2 + w], devs[w]) for w in range(2)],
+                self.RL[q], self.ring_last[q])
 
         def hop1(self, q):
             devs = both_ways(self.axis)
             self.near[q].arrive()
             for w in range(2):
                 chunk = self.half(1 + 2 * w, q, w)
-                add_rows(chunk, [chunk, self.RL.at[q, w]], 2)
+                add_rows(chunk, [chunk, self.RL[q].at[w]], 2)
             Group(
-                [(self.half(1 + 2 * w, q, w), self.RS.at[q, w], devs[w]) for w in range(2)],
-                self.RL.at[q], self.ring_last[q])
+                [(self.half(1 + 2 * w, q, w), self.RS[q].at[w], devs[w]) for w in range(2)],
+                self.RL[q], self.ring_last[q])
 
         def second(self, q):
-            wait_bytes(self.RS.at[q], self.ring_last[q])
+            wait_bytes(self.RS[q], self.ring_last[q])
             for h in range(2):
                 add_rows(
-                    self.S2.at[q, pl.ds(2 * h, 2)], [self.half(0, q, h), self.RS.at[q, h], self.RS.at[q, 3 - h]], 2)
+                    self.S2[q].at[pl.ds(2 * h, 2)], [self.half(0, q, h), self.RS[q].at[h], self.RS[q].at[3 - h]], 2)
             self.two[q] = spread(
-                self.other, lambda r: self.S2.at[q, r], lambda r: self.R2.at[q, r - 1], (2, 1, 3), self.R2.at[q])
+                self.other, lambda r: self.S2[q].at[r], lambda r: self.R2[q].at[r - 1], (2, 1, 3), self.R2[q])
 
         def third(self, q):
             self.two[q].arrive()
-            add_rows(self.S3.at[pl.ds(K * q, K)], [self.S2.at[q, 0]] + [self.R2.at[q, r] for r in range(3)], K)
-            order = [r for r in ORDER[K * q:K * q + K] if r > 0]
+            add_rows(self.S3.at[pl.ds(START[q], GROUPS[q])], [self.S2[q].at[0]] + [self.R2[q].at[r] for r in range(3)], GROUPS[q])
+            order = [r for r in ORDER[START[q]:START[q] + GROUPS[q]] if r > 0]
             spread("z", lambda r: self.S3.at[PLACE[r]], lambda r: self.R3.at[r - 1], order,
-                   self.S3.at[pl.ds(K * q, len(order))], self.three)
+                   self.S3.at[pl.ds(START[q], len(order))], self.three)
 
         def own(self, r):
-            return self.W.at[0, PLACE[r] // K, 0, PLACE[r] % K]
+            return self.W[GROUP[PLACE[r]]].at[0, 0, PLACE[r] - START[GROUP[PLACE[r]]]]
 
         def update(self):
             wait_bytes(self.R3, self.three)
             own_update(self.units, self.S3.at[7], self.R3, 7, self.own(0))
             spread("z", lambda r: self.own(0), lambda r: self.own(NZ - r), near_first, self.R3,
-                   [self.back[PLACE[NZ - r] // K] for r in near_first])
+                   [self.back[GROUP[PLACE[NZ - r]]] for r in near_first])
 
         def across(self, q):
-            came = len([r for r in ORDER[K * q:K * q + K] if r > 0])
-            wait_bytes(self.W.at[0, q, 0, pl.ds(0, came)], self.back[q])
+            came = len([r for r in ORDER[START[q]:START[q] + GROUPS[q]] if r > 0])
+            wait_bytes(self.W[q].at[0, 0, pl.ds(0, came)], self.back[q])
             self.across_[q] = spread(
-                self.other, lambda r: self.W.at[0, q, 0], lambda r: self.W.at[0, q, 4 - r], (2, 1, 3),
-                self.W.at[0, q, pl.ds(1, 3)])
+                self.other, lambda r: self.W[q].at[0, 0], lambda r: self.W[q].at[0, 4 - r], (2, 1, 3),
+                self.W[q].at[0, pl.ds(1, 3)])
 
         def go0(self, q):
             devs = both_ways(self.axis)
             self.across_[q].arrive()
             self.long[q] = Group(
-                [(self.part(0, q, w), self.part(3 - 2 * w, q, w), devs[w]) for w in range(2)], self.W.at[0, q])
+                [(self.part(0, q, w), self.part(3 - 2 * w, q, w), devs[w]) for w in range(2)], self.W[q].at[0])
             Group(
                 [(self.part(0, q, 1 - w), self.part(3 - 2 * w, q, 1 - w), devs[w]) for w in range(2)],
-                self.W.at[0, q], self.gather_last[q])
+                self.W[q].at[0], self.gather_last[q])
 
         def go1(self, q):
             devs = both_ways(self.axis)
             self.long[q].arrive()
             Group(
                 [(self.part(3 - 2 * w, q, w), self.part(2, q, w), devs[w]) for w in range(2)],
-                self.W.at[0, q], self.gather_last[q])
+                self.W[q].at[0], self.gather_last[q])
 
         def finish(self, q):
-            wait_bytes(self.W.at[pl.ds(0, 2), q], self.gather_last[q])
+            if q not in self.done:
+                self.done.add(q)
+                wait_bytes(self.W[q].at[pl.ds(0, 2)], self.gather_last[q])
 
     streams = {name: Stream(name, bufs) for name, bufs in zip(STREAMS, (buf_x, buf_y))}
     x_s, y_s = streams.values()
@@ -415,19 +420,18 @@
             return carry
         lax.fori_loop(0, 8, body, 0)
 
+    v_sem = arrival()
+
     def values(part):
-        blocks = NZ // PARTS
-        first = part * blocks
+        blocks, first = GROUPS[part], START[part]
         for st in streams.values():
-            for q in sorted({(first + i) // K for i in range(blocks)}):
-                st.finish(q)
+            st.finish(part)
         for step in range(max(min(r, NZ - r) for r in ORDER[first:first + blocks])):
             zs["gather", step].arrive()
 
         def body(j, carry):
             y_lo = lax.rem(j, 2)
             k = first + j // 2
-            q, kk = k // K, lax.rem(k, K)
             for g, xr, yr in groups(y_lo):
                 def put(unit, w):
                     row, col = unit
@@ -435,82 +439,79 @@
                     WT[at, col * 128:col * 128 + 128] = w
                 for st in streams.values():
                     for i, unit in enumerate(st.units):
-                        put(unit, st.W[st.places(xr, q, yr, kk, i)])
+                        put(unit, st.W[part][st.places(xr, yr, j // 2, i)])
                 for i, unit in enumerate(Z_UNITS):
                     put(unit, WZ[k, xr, yr, i])
             return carry
         lax.fori_loop(0, 2 * blocks, body, 0)
-        product = jnp.dot(NB[part], WT[...], preferred_element_type=F32)
-        if part == PARTS - 1:
-            VO[...] = product
+        cols, rows = pl.ds(first * 512, blocks * 512), pl.ds(0, blocks * 512)
+        if part == Q - 1:
+            VO[...] = jnp.dot(NB[:, cols], WT[rows, :], preferred_element_type=F32)
+        elif part > 0:
+            VO[...] += jnp.dot(NB[:, cols], WT[rows, :], preferred_element_type=F32)
         else:
-            VO[...] += product
+            theirs, ours = pl.ds(128, 128), pl.ds(0, 128)
+            VO[theirs, :] += jnp.dot(NB[theirs, cols], WT[rows, :], preferred_element_type=F32)
+            Group([(VO.at[theirs], VR, mate)], VR, v_sem)
+            VO[ours, :] += jnp.dot(NB[ours, cols], WT[rows, :], preferred_element_type=F32)
 
     def nexts():
         wait_bytes(NB, bulk_sem.at[2])
 
-    v_sem = arrival()
-
     def last_swap():
-        VS[...] = VO[pl.ds(128, 128), :]
-        Group([(VS, VR, mate)], VR, v_sem)
         wait_bytes(VR, v_sem)
         o_values[...] = (VO[pl.ds(0, 128), :] + VR[...]).astype(BF16)
 
     wait_bytes(CB, c_sem)
     gemm(0, 1)
     z_long(0)
-    gemm(1, 2)
+    y_s.hop0(0)
     x_s.hop0(0)
-    y_s.hop0(0)
-    gemm(2, 3)
-    z_short(0)
-    gemm(3, 4)
-    states()
+    gemm(1, 3)
     x_s.hop0(1)
     y_s.hop0(1)
-    gemm(4, 5)
+    z_short(0)
+    gemm(3, 5)
+    y_s.hop1(0)
+    y_s.hop0(2)
+    x_s.hop1(0)
+    x_s.hop0(2)
     z_long(1)
-    x_s.hop1(0)
-    y_s.hop1(0)
-    gemm(5, 6)
-    y_s.hop0(2)
-    x_s.hop0(2)
+    gemm(5, 8)
+    x_s.hop1(1)
+    states()
     z_short(1)
-    x_s.hop1(1)
-    gemm(6, 7)
     y_s.hop1(1)
+    x_s.hop0(3)
+    y_s.second(0)
+    y_s.hop0(3)
+    x_s.second(0)
+    x_s.hop1(2)
     z_long(2)
-    gemm(7, 8)
-    x_s.hop0(3)
-    x_s.second(0)
-    y_s.hop0(3)
+    y_s.hop1(2)
     z_short(2)
-    x_s.hop1(2)
+    x_s.hop1(3)
     z_long(3)
-    y_s.hop1(2)
+    x_s.second(1)
     y_s.second(1)
-    x_s.hop1(3)
-    x_s.second(1)
+    y_s.hop1(3)
+    y_s.second(2)
+    y_s.third(0)
     x_s.third(0)
-    y_s.second(0)
-    y_s.hop1(3)
-    nexts()
     x_s.second(2)
     z_second()
+    x_s.second(3)
+    y_s.second(3)
+    x_s.third(1)
+    x_s.third(2)
     y_s.third(1)
-    y_s.second(2)
-    x_s.second(3)
-    x_s.third(1)
-    y_s.second(3)
-    y_s.third(0)
-    x_s.third(2)
     z_third()
     x_s.third(3)
     y_s.third(2)
     y_s.third(3)
+    x_s.update()
     z_update()
-    x_s.update()
+    nexts()
     y_s.update()
     rows_1()
     x_s.across(3)
@@ -518,36 +519,36 @@
     x_s.across(2)
     y_s.across(3)
     rows_2()
+    y_s.across(2)
     x_s.across(1)
-    y_s.across(2)
+    z_gather(0)
+    y_s.across(1)
     x_s.go0(3)
     x_s.across(0)
-    z_gather(0)
-    y_s.across(1)
     y_s.go0(3)
     y_s.across(0)
-    x_s.go0(2)
     y_s.go0(2)
+    x_s.go0(1)
     z_gather(1)
     y_s.go0(1)
     rows_3()
-    x_s.go0(1)
-    x_s.go1(3)
-    x_s.go1(2)
-    x_s.go0(0)
+    moments(0)
+    x_s.go0(2)
     y_s.go1(3)
-    y_s.go0(0)
-    z_gather(2)
-    moments(0)
-    x_s.go1(1)
-    y_s.go1(2)
-    y_s.go1(1)
     zs["g3"].arrive()
     moments(1)
-    values(3)
-    y_s.go1(0)
+    y_s.go0(0)
+    x_s.go0(0)
+    y_s.go1(2)
+    x_s.go1(3)
+    z_gather(2)
+    x_s.go1(2)
+    y_s.go1(1)
+    x_s.go1(1)
     z_gather(3)
     x_s.go1(0)
+    y_s.go1(0)
+    values(3)
     values(2)
     values(1)
     values(0)
@@ -556,7 +557,7 @@
         if group is not None:
             group.leave()
     wait_bytes(XB.at[pl.ds(0, 8)], bulk_sem.at[0])
-    wait_bytes(NB.at[pl.ds(0, 2)], bulk_sem.at[1])
+    wait_bytes(NB.at[pl.ds(0, 128)], bulk_sem.at[1])
 
 
 def place(a, b, c, d, o_a, o_b, o_c, o_d, sem):
@@ -581,19 +582,20 @@
 
     def stream_buffers(n):
         u = (n,) + unit
-        return (
-            vm(4, Q, 4, K, *u), vm(Q, 2, 2, K, *u), vm(Q, 4, 2, K, *u), vm(Q, 4, K, *u), vm(Q, 3, K, *u),
-            vm(8, *u), vm(7, *u), vm(4, Q, 4, K, *u))
+        def each(*dims):
+            return tuple(vm(*dims, size, *u) for size in GROUPS)
+
+        return (each(4, 4), each(2, 2), each(4, 2), each(4), each(3), vm(8, *u), vm(7, *u), each(4, 4))
 
     half_z = (2, 4, 2) + unit
     scratch = [
-        vm(16, 1024, 256), vm(1024, 512), vm(4, 256, 1024),
+        vm(16, 1024, 256), vm(1024, 512), vm(256, 4096),
         vm(8, 4, 4, 2, *unit), vm(4, 2, *half_z), vm(3, 2, *half_z),
         vm(4, 4, 2, *unit), vm(3, 4, 2, *unit), vm(4, 2, *unit), vm(3, 2, *unit), vm(8, 4, 4, 2, *unit),
         *[stream_buffers(len(STREAMS[name][2])) for name in STREAMS],
         vm(2, 2, 4, 32, 512),
         vm(3, 512, 512, dtype=F32),
-        vm(1024, 512), vm(256, 512, dtype=F32), vm(128, 512, dtype=F32), vm(128, 512, dtype=F32),
+        vm(512 * max(GROUPS), 512), vm(256, 512, dtype=F32), vm(128, 512, dtype=F32),
         pltpu.SemaphoreType.DMA((POOL,)), pltpu.SemaphoreType.DMA((ARRIVALS,)),
         pltpu.SemaphoreType.DMA((16,)), pltpu.SemaphoreType.DMA((4,)),
     ]

time: 71.3 us -> 70.4 us (0.987)
  Pallas kernels: 70.6 us -> 69.7 us
    pallas_call x1, Pallas kernels: 68.9 us -> 68 us  [local_step(): pl.pallas_call(kernel, out_shape=tuple((pltpu.VMEM(shape, dtype) for shap...]
where the time goes in v4:
time: 70.4 us; the launch traced here: 70.3 us
  Pallas kernels  69.7 us (99%)
    pallas_call x1, Pallas kernels, local_step(): pl.pallas_call(kernel, out_shape=tuple((pltpu.VMEM(shape, dtype) for shap...  68 us
    pallas_call x1, Pallas kernels, local_step(): pl.pallas_call(place, out_shape=tuple((jax.ShapeDtypeStruct(shape, dtype)...  1.73 us

profile of v4, /device:TPU:1, one launch (start us, length us, event | category | flops | bytes accessed | tf_op | source)
XLA Modules:
  0.0 70.3 jit_solution(16439157888957664786)
XLA Ops:
  0.6 68.0 %value_projection_step.1 = (f32[512,512]{1,0:T(8,128)S(1)}, f32[512,512]{1,0:T(8,128)S(1)}, f32[512,512]{1,0:T(8,128)S(1)}, bf16[128,512]{1,0:T(8,128)(2,1)S(1)}) custom-call(bf16[512,8192]{1,0:T(8,128)(2,1)} %x_hbm.1, bf16[512,512]{1,0:T(8,128)(2,1)} %c_hbm.1, f32[512,512]{1,0:T(8,128)} %master_hbm.1, f32[512,512]{1,0:T(8,128)} %first_hbm.1, ...), custom_call_target="tpu_custom_call" | custom-call | flops 5400000000 | bytes 18000000 | tf_op jit(solution)/shard_map/value_projection_step/pallas_call | solution.py:602
  68.6 1.7 %place_results.1 = (f32[512,512]{1,0:T(8,128)}, f32[512,512]{1,0:T(8,128)}, f32[512,512]{1,0:T(8,128)}, bf16[128,512]{1,0:T(8,128)(2,1)}) custom-call(f32[512,512]{1,0:T(8,128)S(1)} %get-tuple-element.8.a, f32[512,512]{1,0:T(8,128)S(1)} %get-tuple-element.9.b, f32[512,512]{1,0:T(8,128)S(1)} %get-tuple-element.10.c, bf16[128,512]{1,0:T(8,128)(2,1)S(1)} %get-tuple-element.11.d), custom_call_target="tpu_custom_call" | custom-call | tf_op jit(solution)/shard_map/place_results/pallas_call | solution.py:613

commit v5 on v4

--- a/solution.py
+++ b/solution.py
@@ -18,8 +18,8 @@
 F32 = jnp.float32
 
 NX, NY, NZ = 4, 4, 8
-POOL = 24
-ARRIVALS = 80
+POOL = 12
+ARRIVALS = 70
 AXES = {"x": NX, "y": NY, "z": NZ}
 ORDER = (4, 3, 5, 2, 6, 1, 7, 0)
 PLACE = {r: k for k, r in enumerate(ORDER)}
@@ -141,11 +141,13 @@
 
     c_sem = arrival()
     pltpu.make_async_copy(c_hbm, CB.at[pl.ds(0, 512)], c_sem).start()
-    each(16, lambda t: x_load(t).start())
+    each(2, lambda t: x_load(t).start())
     pl.semaphore_wait(barrier, len(partners))
 
     Group([(c_hbm, CB.at[pl.ds(512, 512)], mate)], CB.at[pl.ds(512, 512)], c_sem)
-    each(16, lambda t: x_push(t).start())
+    each(4, lambda t: x_push(t).start())
+    each(14, lambda t: x_load(t + 2).start())
+    each(12, lambda t: x_push(t + 4).start())
     for i, ref in enumerate((master_hbm, first_hbm, second_hbm)):
         pltpu.make_async_copy(ref, MFS.at[i], bulk_sem.at[3]).start()
     each(16, lambda t: n_load(t).start())
@@ -264,7 +266,7 @@
         def __init__(self, name, bufs):
             self.axis, self.other, self.units = STREAMS[name]
             self.P, self.RL, self.RS, self.S2, self.R2, self.S3, self.R3, self.W = bufs
-            self.two, self.near, self.across_, self.long = {}, {}, {}, {}
+            self.two, self.near, self.long = {}, {}, {}
             self.ring_last = [arrival() for _ in range(Q)]
             self.gather_last = [arrival() for _ in range(Q)]
             self.back = [arrival() for _ in range(Q)]
@@ -325,13 +327,13 @@
         def across(self, q):
             came = len([r for r in ORDER[START[q]:START[q] + GROUPS[q]] if r > 0])
             wait_bytes(self.W[q].at[0, 0, pl.ds(0, came)], self.back[q])
-            self.across_[q] = spread(
+            spread(
                 self.other, lambda r: self.W[q].at[0, 0], lambda r: self.W[q].at[0, 4 - r], (2, 1, 3),
-                self.W[q].at[0, pl.ds(1, 3)])
+                self.W[q].at[0, pl.ds(1, 3)], self.near[q].recv)
 
         def go0(self, q):
             devs = both_ways(self.axis)
-            self.across_[q].arrive()
+            wait_bytes(self.W[q].at[0, pl.ds(1, 3)], self.near[q].recv)
             self.long[q] = Group(
                 [(self.part(0, q, w), self.part(3 - 2 * w, q, w), devs[w]) for w in range(2)], self.W[q].at[0])
             Group(

time: 70.4 us -> 71 us (level)
  no operation moved by 1% of the time
where the time goes in v5:
time: 71 us
  Pallas kernels  70.3 us (99%)
    pallas_call x1, Pallas kernels, local_step(): pl.pallas_call(kernel, out_shape=tuple((pltpu.VMEM(shape, dtype) for shap...  68.6 us
    pallas_call x1, Pallas kernels, local_step(): pl.pallas_call(place, out_shape=tuple((jax.ShapeDtypeStruct(shape, dtype)...  1.73 us

profile of v5, /device:TPU:1, one launch (start us, length us, event | category | flops | bytes accessed | tf_op | source)
XLA Modules:
  0.0 71.0 jit_solution(17597134557732832850)
XLA Ops:
  0.6 68.6 %value_projection_step.1 = (f32[512,512]{1,0:T(8,128)S(1)}, f32[512,512]{1,0:T(8,128)S(1)}, f32[512,512]{1,0:T(8,128)S(1)}, bf16[128,512]{1,0:T(8,128)(2,1)S(1)}) custom-call(bf16[512,8192]{1,0:T(8,128)(2,1)} %x_hbm.1, bf16[512,512]{1,0:T(8,128)(2,1)} %c_hbm.1, f32[512,512]{1,0:T(8,128)} %master_hbm.1, f32[512,512]{1,0:T(8,128)} %first_hbm.1, ...), custom_call_target="tpu_custom_call" | custom-call | flops 5400000000 | bytes 18000000 | tf_op jit(solution)/shard_map/value_projection_step/pallas_call | solution.py:604
  69.2 1.7 %place_results.1 = (f32[512,512]{1,0:T(8,128)}, f32[512,512]{1,0:T(8,128)}, f32[512,512]{1,0:T(8,128)}, bf16[128,512]{1,0:T(8,128)(2,1)}) custom-call(f32[512,512]{1,0:T(8,128)S(1)} %get-tuple-element.8.a, f32[512,512]{1,0:T(8,128)S(1)} %get-tuple-element.9.b, f32[512,512]{1,0:T(8,128)S(1)} %get-tuple-element.10.c, bf16[128,512]{1,0:T(8,128)(2,1)S(1)} %get-tuple-element.11.d), custom_call_target="tpu_custom_call" | custom-call | tf_op jit(solution)/shard_map/place_results/pallas_call | solution.py:615
